TPU v7x, 128 devices: a whole 4x4x4 slice. The times are simulated.
128 devices in a mesh: row: 16 (over z_hi, x, core), col: 8 (over y, z_lo).
Axes of the slice: x: 4, y: 4, z: 4 (z_hi: 2, z_lo: 2; z = z_hi * 2 + z_lo), core: 2. Of those that a mesh axis runs over, the one named last changes fastest.
Arguments:
- pair: bfloat16 [512, 512, 128], P('row', 'col'), may hold values from -6 to 6
- residue_mask: int32 [512], replicated, may hold values 0 or 1
- in_gain: float32 [2, 128], replicated, may hold values from 0.1 to 1.9
- proj_weight: bfloat16 [2, 128, 512], replicated, may hold values from -0.5 to 0.5
- gate_weight: bfloat16 [2, 128, 128], replicated, may hold values from -0.5 to 0.5
- out_gain: float32 [2, 128], replicated, may hold values from 0.1 to 1.9
- out_weight: bfloat16 [2, 128, 128], replicated, may hold values from -0.5 to 0.5
Outputs:
- updated: bfloat16 [512, 512, 128], P('row', 'col')
Inputs may be any that keep to these rules, and one draw needn't show every extreme that they name: `residue_mask`: 1 marks a present residue.
All inputs are finite; a program needn't handle non-finite values.
Results may differ from a plain program's by a relative error of at most 0.02.
Values may be sent and summed in bfloat16 or wider, within the bound.
A program may use at most 128 MiB of HBM per device.

v0:
```python
import jax
import jax.numpy as jnp
from jax import lax
from jax.sharding import PartitionSpec as P

EPSILON = 1e-05


def broadcast(block, axis, owner):
    block = jnp.where(lax.axis_index(axis) == owner, block, jnp.zeros_like(block))
    return lax.psum(block, axis)


def layer_norm(values, scale_gain):
    values = values.astype(jnp.float32)
    center = jnp.mean(values, axis=-1, keepdims=True)
    spread = jnp.mean(jnp.square(values - center), axis=-1, keepdims=True)
    return (values - center) / jnp.sqrt(spread + EPSILON) * scale_gain


def project_inputs(pair_tile, pair_weight, gain_in, weight_proj, weight_gate):
    normed = layer_norm(pair_tile, gain_in).astype(jnp.bfloat16)
    projected = jnp.dot(normed, weight_proj, preferred_element_type=jnp.float32)
    hidden = weight_proj.shape[1] // 4
    left_proj = (
        jax.nn.sigmoid(projected[..., :hidden]) * projected[..., hidden : 2 * hidden] * pair_weight
    ).astype(jnp.bfloat16)
    right_proj = (
        jax.nn.sigmoid(projected[..., 2 * hidden : 3 * hidden])
        * projected[..., 3 * hidden :]
        * pair_weight
    ).astype(jnp.bfloat16)
    gate_value = jax.nn.sigmoid(
        jnp.dot(normed, weight_gate, preferred_element_type=jnp.float32)
    ).astype(jnp.bfloat16)
    return (left_proj, right_proj, gate_value)


def finish_update(pair_tile, product, gate_value, gain_out, weight_out):
    normout = layer_norm(product, gain_out).astype(jnp.bfloat16)
    update = jnp.dot(normout, weight_out, preferred_element_type=jnp.float32)
    return (pair_tile.astype(jnp.float32) + gate_value.astype(jnp.float32) * update).astype(
        jnp.bfloat16
    )


def shards(pair, residue_mask, in_gain, proj_weight, gate_weight, out_gain, out_weight):
    rows_here = pair.shape[0]
    cols_here = pair.shape[1]
    row_index = lax.axis_index("row")
    col_index = lax.axis_index("col")
    row_flags = lax.dynamic_slice_in_dim(residue_mask, row_index * rows_here, rows_here).astype(
        jnp.float32
    )
    col_flags = lax.dynamic_slice_in_dim(residue_mask, col_index * cols_here, cols_here).astype(
        jnp.float32
    )
    pair_weight = (row_flags[:, None] * col_flags[None, :])[:, :, None]
    left_out, right_out, gate_out = project_inputs(
        pair, pair_weight, in_gain[0], proj_weight[0], gate_weight[0]
    )
    right_all = lax.all_gather(right_out, "row", axis=0, tiled=True)
    summed = lax.psum_scatter(
        jnp.einsum("ikc,jkc->jic", left_out, right_all, preferred_element_type=jnp.float32).astype(
            jnp.bfloat16
        ),
        "col",
        scatter_dimension=0,
        tiled=True,
    ).astype(jnp.float32)
    product_out = jnp.transpose(summed, (1, 0, 2))
    middle = finish_update(pair, product_out, gate_out, out_gain[0], out_weight[0])
    left_in, right_in, gate_in = project_inputs(
        middle, pair_weight, in_gain[1], proj_weight[1], gate_weight[1]
    )
    left_all, right_all_in = (
        lax.all_gather(left_in, "row", axis=0, tiled=True),
        lax.all_gather(right_in, "row", axis=0, tiled=True),
    )
    root_col = row_index * rows_here // cols_here
    offset = row_index * rows_here - root_col * cols_here
    picked_cols = lax.dynamic_slice_in_dim(left_all, offset, rows_here, 1)
    left_cols = broadcast(picked_cols, "col", root_col)
    product_in = jnp.einsum(
        "kic,kjc->ijc", left_cols, right_all_in, preferred_element_type=jnp.float32
    )
    return finish_update(middle, product_in, gate_in, out_gain[1], out_weight[1])


def solution(mesh):
    placed = (P("row", "col", None), P(), P(), P(), P(), P(), P())
    return jax.shard_map(
        shards, mesh=mesh, in_specs=placed, out_specs=P("row", "col", None), check_vma=False
    )
```

profile of v0, /device:TPU:1, one launch (start us, length us, event | category | flops | bytes accessed | tf_op | source)
XLA Modules:
  0.0 578.8 jit_solution(6375810767305250811)
XLA Ops:
  8.0 1.4 convert_reduce_fusion.1
  9.4 1.7 fusion.19
  12.0 2.0 fusion.51
  14.0 1.4 fusion.33
  15.5 1.6 copy.37
  17.1 74.9 %all-gather.4.cloned.1.call-done = bf16[512,64,128]{2,1,0:T(8,128)(2,1)} async-done(((bf16[32,64,128]{2,1,0:T(8,128)(2,1)}), bf16[512,64,128]{2,1,0:T(8,128)(2,1)}) %all-gather.4.cloned.1.call-update) | async-done | bytes 8388624 | tf_op jit(solution)/shard_map/all_gather | solution.py:62
  92.0 23.7 %copy.36 = bf16[512,64,128]{1,0,2:T(8,128)(2,1)} copy(bf16[512,64,128]{2,1,0:T(8,128)(2,1)} %all-gather.4.cloned.1.call-done) | data formatting | bytes 16777216 | tf_op jit(solution)/shard_map/all_gather | solution.py:62
  115.7 10.7 %convert_bitcast_fusion = bf16[512,32,128]{0,1,2:T(8,128)(2,1)} fusion(bf16[512,64,128]{1,0,2:T(8,128)(2,1)} %copy.36, bf16[32,64,128]{1,0,2:T(8,128)(2,1)S(1)} %copy.37), kind=kOutput, calls=%fused_computation | convolution fusion | flops 270532608 | bytes 13107200 | tf_op jit(solution)/shard_map/ikc,jkc->jic/dot_general | solution.py:64
  126.4 9.1 %copy.38 = bf16[512,32,128]{2,1,0:T(8,128)(2,1)} copy(bf16[512,32,128]{0,1,2:T(8,128)(2,1)} %convert_bitcast_fusion) | data formatting | bytes 8388608 | tf_op jit(solution)/shard_map/convert_element_type | solution.py:64
  137.3 85.9 %reduce-scatter.2.cloned.1.call-done = bf16[64,32,128]{2,1,0:T(8,128)(2,1)} async-done(((bf16[512,32,128]{2,1,0:T(8,128)(2,1)}), bf16[64,32,128]{2,1,0:T(8,128)(2,1)}) %reduce-scatter.2.cloned.1.call-update) | async-done | bytes 524304 | tf_op jit(solution)/shard_map/reduce_scatter | solution.py:63
  223.3 1.4 bitcast_reduce_fusion.1
  224.8 1.7 fusion.44
  226.7 1.7 fusion.46
  229.6 0.8 fusion.49
  230.4 1.6 fusion.23
  232.8 73.4 %all-gather.8.cloned.1.call-done = bf16[512,64,128]{2,1,0:T(8,128)(2,1)} async-done(((bf16[32,64,128]{2,1,0:T(8,128)(2,1)}), bf16[512,64,128]{2,1,0:T(8,128)(2,1)}) %all-gather.8.cloned.1.call-update) | async-done | bytes 8388624 | tf_op jit(solution)/shard_map/all_gather | solution.py:77
  306.2 4.9 constant_dynamic-slice_fusion
  311.2 8.7 %copy.47 = bf16[512,32,128]{0,1,2:T(8,128)(2,1)} copy(bf16[512,32,128]{2,1,0:T(8,128)(2,1)} %constant_dynamic-slice_fusion) | data formatting | bytes 8388608
  319.8 4.4 broadcast_select_fusion
  325.1 53.9 %all-gather.6.cloned.1.call-done = bf16[512,64,128]{2,1,0:T(8,128)(2,1)} async-done(((bf16[32,64,128]{2,1,0:T(8,128)(2,1)}), bf16[512,64,128]{2,1,0:T(8,128)(2,1)}) %all-gather.6.cloned.1.call-update) | async-done | bytes 8388624 | tf_op jit(solution)/shard_map/all_gather | solution.py:78
  379.0 23.8 %copy.45 = bf16[512,64,128]{1,0,2:T(8,128)(2,1)} copy(bf16[512,64,128]{2,1,0:T(8,128)(2,1)} %all-gather.6.cloned.1.call-done) | data formatting | bytes 16777216 | tf_op jit(solution)/shard_map/all_gather | solution.py:78
  402.8 157.8 %all-reduce.2.cloned.1.call-done = bf16[512,32,128]{0,1,2:T(8,128)(2,1)} async-done(((bf16[512,32,128]{0,1,2:T(8,128)(2,1)}), bf16[512,32,128]{0,1,2:T(8,128)(2,1)}) %all-reduce.2.cloned.1.call-update) | async-done | bytes 4194320 | tf_op jit(solution)/shard_map/psum | solution.py:11
  560.6 9.7 %bitcast_reduce_fusion = (f32[32,64]{1,0:T(8,128)S(1)}, f32[128,64,32]{1,2,0:T(8,128)S(1)}) fusion(bf16[512,32,128]{0,1,2:T(8,128)(2,1)} %all-reduce.2.cloned.1.call-done, bf16[512,64,128]{1,0,2:T(8,128)(2,1)} %copy.45), kind=kOutput, calls=%fused_computation.3 | convolution fusion | flops 268695552 | bytes 13639680 | tf_op jit(solution)/shard_map/kic,kjc->ijc/dot_general | solution.py:84
  570.9 1.4 fusion.6
  (43 shorter events, 7.9 us)
Async XLA Ops:
  6.5 85.4 %all-gather.4.cloned.1.call-start = ((), (), s32[]{:S(2)}) async-start(), calls=%async_computation.1 | async-start | bytes 8912896 | tf_op jit(solution)/shard_map/all_gather | solution.py:62
  15.4 207.9 %reduce-scatter.2.cloned.1.call-start = ((), (), s32[]{:S(2)}) async-start(), calls=%async_computation.2 | async-start | bytes 4718592 | tf_op jit(solution)/shard_map/reduce_scatter | solution.py:63
  135.5 0.7 copy-start.3
  135.5 1.1 copy-start
  135.5 1.1 copy-start.4
  135.5 170.7 %all-gather.8.cloned.1.call-start = ((), (), s32[]{:S(2)}) async-start(), calls=%async_computation.4 | async-start | bytes 8912896 | tf_op jit(solution)/shard_map/all_gather | solution.py:77
  136.6 91.8 %copy-start.2 = (bf16[2,128,128]{2,1,0:T(8,128)(2,1)S(1)}, bf16[2,128,128]{2,1,0:T(8,128)(2,1)}, u32[]{:S(2)}) copy-start(bf16[2,128,128]{2,1,0:T(8,128)(2,1)} %param.13) | copy-start | bytes 196612
  137.3 92.3 %copy-start.1 = (bf16[2,128,512]{2,1,0:T(8,128)(2,1)S(1)}, bf16[2,128,512]{2,1,0:T(8,128)(2,1)}, u32[]{:S(2)}) copy-start(bf16[2,128,512]{2,1,0:T(8,128)(2,1)} %param.10) | copy-start | bytes 786436
  232.0 147.0 %all-gather.6.cloned.1.call-start = ((), (), s32[]{:S(2)}) async-start(), calls=%async_computation.3 | async-start | bytes 8912896 | tf_op jit(solution)/shard_map/all_gather | solution.py:78
  232.6 328.0 %all-reduce.2.cloned.1.call-start = ((), (), s32[]{:S(2)}) async-start(), calls=%async_computation.5 | async-start | bytes 8388608 | tf_op jit(solution)/shard_map/psum | solution.py:11
Sparse Core Ops, SparseCore 0:
  15.5 76.3 all-gather.3
  135.7 87.5 reduce-scatter.1
  232.1 74.0 all-gather.7
  308.5 70.4 all-gather.5
  381.4 179.1 all-reduce.1
where the time goes:
time: 581 us; the launch traced here: 579 us
  waiting for transfers between devices  446 us (77%)
  local copies, waits for them, and re-layouts  73.9 us (13%)
  matrix products  26.5 us (5%)
  other arithmetic  18.2 us (3%)
  between operations  13.3 us (2%)
    psum x1, waiting for transfers between devices, broadcast(): return lax.psum(block, axis)  158 us
    reduce_scatter x1, waiting for transfers between devices, shards(): lax.psum_scatter(jnp.einsum('ikc,jkc->jic', left_out, right_all, preferre...  85.9 us
    all_gather x1, waiting for transfers between devices, shards(): right_all = lax.all_gather(right_out, 'row', axis=0, tiled=True)  74.9 us
    all_gather x1, waiting for transfers between devices, shards(): lax.all_gather(left_in, 'row', axis=0, tiled=True)  73.4 us
    all_gather x1, waiting for transfers between devices, shards(): lax.all_gather(right_in, 'row', axis=0, tiled=True)  53.9 us
    all_gather x1, local copies, waits for them, and re-layouts, shards(): lax.all_gather(right_in, 'row', axis=0, tiled=True)  23.8 us
    all_gather x1, local copies, waits for them, and re-layouts, shards(): right_all = lax.all_gather(right_out, 'row', axis=0, tiled=True)  23.7 us
  transfers between devices with their start and end apart: 5, of which 5 were waited for; matrix products, arithmetic and copies ran while one was open for 8% of the time, Pallas kernels for 0%

commit v1 on v0

v1 whole, which is shorter than its diff:
```python
import jax
import jax.numpy as jnp
from jax import lax
from jax.experimental import pallas as pl
from jax.experimental.pallas import tpu as pltpu
from jax.sharding import PartitionSpec as P

EPSILON = 1e-05
MESH = pl.DeviceIdType.MESH
DEVICES = 128
C = 128
ROWS = 32
COLS = 64
HALF = ROWS // 2
TILES = 16


def coords():
    r = lax.axis_index("row")
    c = lax.axis_index("col")
    return lax.rem(r // 2, 4), c // 2, (r // 8) * 2 + lax.rem(c, 2), lax.rem(r, 2)


def device_at(x, y, z, k):
    return ((z // 2) * 8 + x * 2 + k, y * 2 + lax.rem(z, 2))


def wrap(a):
    return lax.rem(a + 4, 4)


def enter(stage_sem):
    x, y, z, k = coords()
    xs = [device_at(wrap(x + a), y, z, k) for a in (1, 2, 3)]
    ys = [device_at(x, wrap(y + a), z, k) for a in (1, 2, 3)]
    zs = [device_at(x, y, wrap(z + a), k) for a in (1, 2, 3)]
    ks = [device_at(x, y, z, 1 - k)]
    barrier = pltpu.get_barrier_semaphore()
    for peer in xs + ys + zs + ks:
        pl.semaphore_signal(barrier, inc=1, device_id=peer, device_id_type=MESH)
    pl.semaphore_wait(barrier, 10)
    for stage, peers in enumerate((ys, zs, ks)):
        for peer in peers:
            pl.semaphore_signal(stage_sem.at[stage], inc=1, device_id=peer, device_id_type=MESH)
        pl.semaphore_wait(stage_sem.at[stage], len(peers))


def exchange(send, recv, send_sem, recv_sem):
    x, y, z, k = coords()
    me = lax.axis_index("row") * 8 + lax.axis_index("col")

    def step(s, carry):
        dx, dy, dz, dk = lax.rem(s, 4), lax.rem(s // 4, 4), lax.rem(s // 16, 4), s // 64
        row, col = device_at(wrap(x + dx), wrap(y + dy), wrap(z + dz), lax.rem(k + dk, 2))
        pltpu.make_async_remote_copy(
            send.at[row * 8 + col],
            recv.at[me],
            send_sem,
            recv_sem,
            device_id=(row, col),
            device_id_type=MESH,
        ).start()
        return carry

    lax.fori_loop(1, DEVICES, step, 0)
    recv[me] = send[me]


def wait_bytes(buffer, sem):
    part = buffer.at[pl.ds(0, DEVICES - 1)]
    pltpu.make_async_copy(part, part, sem).wait()


def normalise(values, gain):
    center = jnp.mean(values, axis=0, keepdims=True)
    moved = values - center
    spread = jnp.mean(moved * moved, axis=0, keepdims=True)
    return moved * lax.rsqrt(spread + EPSILON) * gain


def kernel(
    mask_ref,
    pair_ref,
    in_gain_ref,
    proj_ref,
    gate_ref,
    out_gain_ref,
    outw_ref,
    out_ref,
    proj_t,
    outw_t,
    in_gain_t,
    out_gain_t,
    weight_of,
    state,
    gate,
    left_f,
    right_f,
    sides_s,
    sides_r,
    prod_s,
    prod_r,
    left_m,
    right_m,
    stage_sem,
    send_sem,
    recv_sem,
):
    row_index = lax.axis_index("row")
    col_index = lax.axis_index("col")
    enter(stage_sem)

    lane = lax.broadcasted_iota(jnp.int32, (8, 128), 1)
    low = lane < COLS
    lane_col = lax.rem(lane, COLS)

    def add_col(j, flags):
        return jnp.where(lane_col == j, mask_ref[col_index * COLS + j].astype(jnp.float32), flags)

    col_flags = lax.fori_loop(0, COLS, add_col, jnp.zeros((8, 128), jnp.float32))
    for t in range(TILES):
        upper = mask_ref[row_index * ROWS + t].astype(jnp.float32)
        lower = mask_ref[row_index * ROWS + HALF + t].astype(jnp.float32)
        weight_of[t] = col_flags * jnp.where(low, upper, lower)

    for u in range(2):
        for n in range(4):
            block = proj_ref[u, :, n * 128 : (n + 1) * 128].astype(jnp.float32)
            proj_t[u, n * 128 : (n + 1) * 128, :] = block.T.astype(jnp.bfloat16)
        proj_t[u, 512:640, :] = gate_ref[u].astype(jnp.float32).T.astype(jnp.bfloat16)
        outw_t[u] = outw_ref[u].astype(jnp.float32).T.astype(jnp.bfloat16)
        in_gain_t[u] = jnp.broadcast_to(in_gain_ref[u : u + 1, :], (128, 128)).T
        out_gain_t[u] = jnp.broadcast_to(out_gain_ref[u : u + 1, :], (128, 128)).T

    def project(u, t, values):
        normed = normalise(values, in_gain_t[u]).astype(jnp.bfloat16)
        projected = jnp.dot(proj_t[u], normed, preferred_element_type=jnp.float32)
        weight = weight_of[t][0:1, :]
        left = jax.nn.sigmoid(projected[0:128]) * projected[128:256] * weight
        right = jax.nn.sigmoid(projected[256:384]) * projected[384:512] * weight
        left_f[pl.ds(t, C, stride=TILES), :] = left
        right_f[pl.ds(t, C, stride=TILES), :] = right
        gate[t] = jax.nn.sigmoid(projected[512:640])

    def pack(u):
        def step(c, carry):
            at = pl.ds(pl.multiple_of(c * TILES, TILES), TILES)
            sides_s[u, c, 0:16, :] = left_f[at, :].astype(jnp.bfloat16)
            sides_s[u, c, 16:32, :] = right_f[at, :].astype(jnp.bfloat16)
            return carry

        lax.fori_loop(0, C, step, 0)

    def first(t, carry):
        block = jnp.concatenate([pair_ref[t], pair_ref[t + HALF]], axis=0).astype(jnp.float32).T
        state[t] = block
        project(0, t, block)
        return carry

    lax.fori_loop(0, TILES, first, 0)

    low16 = lax.broadcasted_iota(jnp.int32, (16, 128), 1) < COLS

    def swap(a, b):
        a = a.astype(jnp.float32)
        b = b.astype(jnp.float32)
        one = jnp.where(low16, a, pltpu.roll(b, COLS, 1))
        two = jnp.where(low16, pltpu.roll(a, COLS, 1), b)
        return one.astype(jnp.bfloat16), two.astype(jnp.bfloat16)

    for u in range(2):
        pack(u)
        exchange(sides_s.at[u], sides_r.at[u], send_sem.at[2 * u], recv_sem.at[2 * u])
        wait_bytes(sides_r.at[u], recv_sem.at[2 * u])

        def assemble(r, carry):
            at = pl.multiple_of(r * ROWS, ROWS)
            for m in range(4):
                for side, whole in ((0, left_m), (16, right_m)):
                    one, two = swap(
                        sides_r[u, r * 8 + 2 * m, side : side + 16, :],
                        sides_r[u, r * 8 + 2 * m + 1, side : side + 16, :],
                    )
                    whole[pl.ds(at, 16), m * 128 : (m + 1) * 128] = one
                    whole[pl.ds(at + 16, 16), m * 128 : (m + 1) * 128] = two
            return carry

        lax.fori_loop(0, 16, assemble, 0)
        for q in range(4):
            if u == 0:
                dims = (((1,), (1,)), ((), ()))
                part = left_m[q * 128 : (q + 1) * 128, :]
            else:
                dims = (((0,), (0,)), ((), ()))
                part = left_m[:, q * 128 : (q + 1) * 128]
            product = lax.dot_general(part, right_m[...], dims, preferred_element_type=jnp.float32)
            for r in range(4):
                for m in range(4):
                    one, two = swap(
                        product[r * 32 : r * 32 + 16, m * 128 : (m + 1) * 128],
                        product[r * 32 + 16 : r * 32 + 32, m * 128 : (m + 1) * 128],
                    )
                    prod_s[u, (q * 4 + r) * 8 + 2 * m] = one
                    prod_s[u, (q * 4 + r) * 8 + 2 * m + 1] = two
        exchange(prod_s.at[u], prod_r.at[u], send_sem.at[2 * u + 1], recv_sem.at[2 * u + 1])
        wait_bytes(prod_r.at[u], recv_sem.at[2 * u + 1])

        def unpack(c, carry):
            left_f[pl.ds(pl.multiple_of(c * TILES, TILES), TILES), :] = prod_r[u, c].astype(jnp.float32)
            return carry

        lax.fori_loop(0, C, unpack, 0)

        def finish(t, carry):
            product = left_f[pl.ds(t, C, stride=TILES), :]
            normout = normalise(product, out_gain_t[u]).astype(jnp.bfloat16)
            update = jnp.dot(outw_t[u], normout, preferred_element_type=jnp.float32)
            new = (state[t] + gate[t] * update).astype(jnp.bfloat16).astype(jnp.float32)
            if u == 0:
                state[t] = new
            else:
                back = new.T.astype(jnp.bfloat16)
                out_ref[t] = back[0:COLS]
                out_ref[t + HALF] = back[COLS : 2 * COLS]
            return carry

        lax.fori_loop(0, TILES, finish, 0)
        if u == 0:

            def second(t, carry):
                project(1, t, state[t])
                return carry

            lax.fori_loop(0, TILES, second, 0)

    for u in range(2):
        wait_bytes(sides_s.at[u], send_sem.at[2 * u])
        wait_bytes(prod_s.at[u], send_sem.at[2 * u + 1])


def shards(pair, residue_mask, in_gain, proj_weight, gate_weight, out_gain, out_weight):
    vmem = pl.BlockSpec(memory_space=pltpu.VMEM)
    return pl.pallas_call(
        kernel,
        out_shape=jax.ShapeDtypeStruct(pair.shape, pair.dtype),
        in_specs=[pl.BlockSpec(memory_space=pltpu.SMEM)] + [vmem] * 6,
        out_specs=vmem,
        scratch_shapes=[
            pltpu.VMEM((2, 640, 128), jnp.bfloat16),
            pltpu.VMEM((2, 128, 128), jnp.bfloat16),
            pltpu.VMEM((2, 128, 128), jnp.float32),
            pltpu.VMEM((2, 128, 128), jnp.float32),
            pltpu.VMEM((TILES, 8, 128), jnp.float32),
            pltpu.VMEM((TILES, 128, 128), jnp.float32),
            pltpu.VMEM((TILES, 128, 128), jnp.float32),
            pltpu.VMEM((C * TILES, 128), jnp.float32),
            pltpu.VMEM((C * TILES, 128), jnp.float32),
            pltpu.VMEM((2, DEVICES, 32, 128), jnp.bfloat16),
            pltpu.VMEM((2, DEVICES, 32, 128), jnp.bfloat16),
            pltpu.VMEM((2, DEVICES, 16, 128), jnp.bfloat16),
            pltpu.VMEM((2, DEVICES, 16, 128), jnp.bfloat16),
            pltpu.VMEM((512, 512), jnp.bfloat16),
            pltpu.VMEM((512, 512), jnp.bfloat16),
            pltpu.SemaphoreType.REGULAR((3,)),
            pltpu.SemaphoreType.DMA((4,)),
            pltpu.SemaphoreType.DMA((4,)),
        ],
        compiler_params=pltpu.CompilerParams(
            collective_id=0, has_side_effects=True, vmem_limit_bytes=48 * 1024 * 1024
        ),
    )(residue_mask, pair, in_gain, proj_weight, gate_weight, out_gain, out_weight)


def solution(mesh):
    placed = (P("row", "col", None), P(), P(), P(), P(), P(), P())
    return jax.shard_map(
        shards, mesh=mesh, in_specs=placed, out_specs=P("row", "col", None), check_vma=False
    )
```

time: 581 us -> 100 us (0.17)
  waiting for transfers between devices: 446 us -> 0 us
  Pallas kernels: 0 us -> 93.4 us
  local copies, waits for them, and re-layouts: 73.9 us -> 6.5 us
  matrix products: 26.5 us -> 0 us
  other arithmetic: 18.2 us -> 0 us
  between operations: 13.3 us -> 0.02 us
    all_gather x3 -> x0, waiting for transfers between devices: 202 us -> none  [the longest x1 74.9 us: shards(): right_all = lax.all_gather(right_out, 'row', axis=0, tiled=True)]
    psum x1 -> x0, waiting for transfers between devices: 158 us -> none  [broadcast(): return lax.psum(block, axis)]
    pallas_call x0 -> x1, Pallas kernels: none -> 93.4 us  [shards(): pl.pallas_call(kernel, out_shape=jax.ShapeDtypeStruct(pair.shape, pair.dt...]
    reduce_scatter x1 -> x0, waiting for transfers between devices: 85.9 us -> none  [shards(): lax.psum_scatter(jnp.einsum('ikc,jkc->jic', left_out, right_all, preferre...]
    all_gather x2 -> x0, local copies, waits for them, and re-layouts: 47.5 us -> none  [the longest x1 23.8 us: shards(): lax.all_gather(right_in, 'row', axis=0, tiled=True)]
    dot_general x8 -> x0, matrix products: 26.5 us -> none  [the longest x1 10.7 us: shards(): jnp.einsum('ikc,jkc->jic', left_out, right_all, preferred_element_type=jn...]
    convert_element_type x2 -> x0, local copies, waits for them, and re-layouts: 10.8 us -> none  [the longest x1 9.13 us: shards(): jnp.einsum('ikc,jkc->jic', left_out, right_all, preferred_element_type=jn...]
    reduce_sum x6 -> x0, other arithmetic: 7.11 us -> none  [the longest x4 4.34 us: layer_norm(): spread = jnp.mean(jnp.square(values - center), axis=-1, keepdims=True)]
  transfers between devices with their start and end apart: 5 -> 0, of which waited for: 5 -> 0; matrix products, arithmetic and copies ran while one was open for 8% -> 0% of each run, Pallas kernels for 0% -> 0%
where the time goes in v1:
time: 100 us; the launch traced here: 99.9 us
  Pallas kernels  93.4 us (93%)
  local copies, waits for them, and re-layouts  6.5 us (6%)
    pallas_call x1, Pallas kernels, shards(): pl.pallas_call(kernel, out_shape=jax.ShapeDtypeStruct(pair.shape, pair.dt...  93.4 us
    unnamed x15, local copies, waits for them, and re-layouts  6.5 us

profile of v1, /device:TPU:1, one launch (start us, length us, event | category | flops | bytes accessed | tf_op | source)
XLA Modules:
  0.0 99.9 jit_solution(11705569811579983731)
XLA Ops:
  0.0 0.0 copy-start
  0.0 1.0 %copy-done = bf16[32,64,128]{2,1,0:T(8,128)(2,1)S(1)} copy-done((bf16[32,64,128]{2,1,0:T(8,128)(2,1)S(1)}, bf16[32,64,128]{2,1,0:T(8,128)(2,1)}, u32[]{:S(2)}) %copy-start) | copy-done | bytes 524312
  1.0 0.0 copy-start.1
  1.0 0.9 copy-done.1
  2.0 0.0 copy-start.2
  2.0 0.8 copy-done.2
  2.8 0.0 copy-start.3
  2.8 0.8 copy-done.3
  3.7 0.0 copy-start.4
  3.7 0.7 copy-done.4
  4.4 0.0 copy-start.5
  4.4 0.7 copy-done.5
  5.0 0.0 copy-start.6
  5.0 0.7 copy-done.6
  5.7 93.4 %shard_map.73 = bf16[32,64,128]{2,1,0:T(8,128)(2,1)S(1)} custom-call(s32[512]{0:T(512)S(1)} %copy-done.4, bf16[32,64,128]{2,1,0:T(8,128)(2,1)S(1)} %copy-done, f32[2,128]{1,0:T(2,128)S(1)} %copy-done.5, bf16[2,128,512]{2,1,0:T(8,128)(2,1)S(1)} %copy-done.1, bf16[2,128,128]{2,1,0:T(8,128)(2,1)S(1)} %copy-done.2, f32[2,128]{1,0:T(2,128)S(1)} %copy-done.6, ...), custom_call_target="tpu_custom_call" | custom-call | tf_op jit(solution)/shard_map/pallas_call | solution.py:243
  99.1 0.8 copy.9
Async XLA Ops:
  0.0 1.0 %copy-start = (bf16[32,64,128]{2,1,0:T(8,128)(2,1)S(1)}, bf16[32,64,128]{2,1,0:T(8,128)(2,1)}, u32[]{:S(2)}) copy-start(bf16[32,64,128]{2,1,0:T(8,128)(2,1)} %pair_ref.1) | copy-start | bytes 1572868
  1.0 0.9 copy-start.1
  2.0 0.8 copy-start.2
  2.8 0.8 copy-start.3
  3.7 0.7 copy-start.4
  4.4 0.7 copy-start.5
  5.0 0.7 copy-start.6

commit v2 on v1

v2 whole, which is shorter than its diff:
```python
import jax
import jax.numpy as jnp
from jax import lax
from jax.experimental import pallas as pl
from jax.experimental.pallas import tpu as pltpu
from jax.sharding import PartitionSpec as P

EPSILON = 1e-05
MESH = pl.DeviceIdType.MESH
DEVICES = 128
C = 128
ROWS = 32
COLS = 64
HALF = ROWS // 2
TILES = 16
PAIRS = 8
PARTS = 2


def coords():
    r = lax.axis_index("row")
    c = lax.axis_index("col")
    return lax.rem(r // 2, 4), c // 2, (r // 8) * 2 + lax.rem(c, 2), lax.rem(r, 2)


def device_at(x, y, z, k):
    return ((z // 2) * 8 + x * 2 + k, y * 2 + lax.rem(z, 2))


def wrap(a):
    return lax.rem(a + 4, 4)


def far_first(q):
    return jnp.where(q == 0, 2, jnp.where(q == 3, 0, q * 2 - 1))


def peer_at(s):
    x, y, z, _ = coords()
    a, b, c = lax.rem(s, 4), lax.rem(s // 4, 4), s // 16
    dx = far_first(a)
    dy = far_first(lax.rem(a + b, 4))
    dz = far_first(lax.rem(a + b + c, 4))
    return wrap(x + dx), wrap(y + dy), wrap(z + dz)


def greet():
    barrier = pltpu.get_barrier_semaphore()
    me = lax.axis_index("row") * 8 + lax.axis_index("col")

    def step(s, carry):
        peer = lax.rem(me + s, DEVICES)
        pl.semaphore_signal(
            barrier, inc=1, device_id=(peer // 8, lax.rem(peer, 8)), device_id_type=MESH
        )
        return carry

    lax.fori_loop(1, DEVICES, step, 0)


def send_all(send, recv, send_sem, recv_sem, core):
    _, _, _, k = coords()
    me = lax.axis_index("row") * 8 + lax.axis_index("col")

    def one(s):
        row, col = device_at(*peer_at(s), core)
        pltpu.make_async_remote_copy(
            send.at[row * 8 + col],
            recv.at[me],
            send_sem,
            recv_sem,
            device_id=(row, col),
            device_id_type=MESH,
        ).start()

    def step(s, carry):
        one(s)
        return carry

    lax.fori_loop(0, HERE, step, 0)
    lax.fori_loop(HERE + 1, 64, step, 0)

    @pl.when(k == core)
    def _():
        pltpu.make_async_copy(send.at[me], recv.at[me], recv_sem).start()

    @pl.when(k != core)
    def _():
        one(HERE)


def number_here():
    for s in range(64):
        a, b, c = s % 4, s // 4 % 4, s // 16
        order = (2, 1, 3, 0)
        if order[a] == order[(a + b) % 4] == order[(a + b + c) % 4] == 0:
            return s


HERE = number_here()


def wait_bytes(buffer, sem, count):
    part = buffer.at[pl.ds(0, count)]
    pltpu.make_async_copy(part, part, sem).wait()


def sigmoid(v):
    return 0.5 * jnp.tanh(0.5 * v) + 0.5


def normalise(values, gain):
    center = jnp.mean(values, axis=0, keepdims=True)
    moved = values - center
    spread = jnp.mean(moved * moved, axis=0, keepdims=True)
    return moved * lax.rsqrt(spread + EPSILON) * gain


def kernel(
    mask_hbm,
    pair_hbm,
    in_gain_hbm,
    proj_hbm,
    gate_hbm,
    out_gain_hbm,
    outw_hbm,
    out_ref,
    mask_ref,
    pair_ref,
    in_gain_ref,
    proj_ref,
    gate_ref,
    out_gain_ref,
    outw_ref,
    proj_t,
    outw_t,
    in_gain_t,
    out_gain_t,
    weight_of,
    state,
    gate,
    left_f,
    right_f,
    sides_s,
    sides_r,
    prod_s,
    prod_r,
    left_m,
    right_m,
    in_sem,
    send_sem,
    recv_sem,
):
    row_index = lax.axis_index("row")
    col_index = lax.axis_index("col")
    _, _, _, core = coords()
    loads = [
        pltpu.make_async_copy(source, target, in_sem.at[n])
        for n, (source, target) in enumerate(
            (
                (mask_hbm, mask_ref),
                (proj_hbm, proj_ref),
                (gate_hbm, gate_ref),
                (in_gain_hbm, in_gain_ref),
                (pair_hbm, pair_ref),
                (out_gain_hbm, out_gain_ref),
                (outw_hbm, outw_ref),
            )
        )
    ]
    for load in loads:
        load.start()
    greet()

    def turn(u):
        for n in range(4):
            block = proj_ref[u, :, n * 128 : (n + 1) * 128].astype(jnp.float32)
            proj_t[u, n * 128 : (n + 1) * 128, :] = block.T.astype(jnp.bfloat16)
        proj_t[u, 512:640, :] = gate_ref[u].astype(jnp.float32).T.astype(jnp.bfloat16)
        in_gain_t[u] = jnp.broadcast_to(in_gain_ref[u : u + 1, :], (128, 128)).T

    def turn_out(u):
        outw_t[u] = outw_ref[u].astype(jnp.float32).T.astype(jnp.bfloat16)
        out_gain_t[u] = jnp.broadcast_to(out_gain_ref[u : u + 1, :], (128, 128)).T

    loads[0].wait()
    lane = lax.broadcasted_iota(jnp.int32, (8, 128), 1)
    low = lane < COLS
    lane_col = lax.rem(lane, COLS)
    col_flags = jnp.zeros((8, 128), jnp.float32)
    for j in range(COLS):
        flag = mask_ref[col_index * COLS + j].astype(jnp.float32)
        col_flags = jnp.where(lane_col == j, flag, col_flags)
    for t in range(TILES):
        upper = mask_ref[row_index * ROWS + t].astype(jnp.float32)
        lower = mask_ref[row_index * ROWS + HALF + t].astype(jnp.float32)
        weight_of[t // 2, :, t % 2 * 128 : t % 2 * 128 + 128] = col_flags * jnp.where(low, upper, lower)
    for n in (1, 2, 3):
        loads[n].wait()
    turn(0)
    loads[4].wait()

    def wide(column):
        return jnp.concatenate([column, column], axis=1)

    def project(u, p, values):
        normed = normalise(values, wide(in_gain_t[u])).astype(jnp.bfloat16)
        weight = weight_of[p][0:1, :]

        def times(n):
            return jnp.dot(
                proj_t[u, n * 128 : (n + 1) * 128, :], normed, preferred_element_type=jnp.float32
            )

        left = sigmoid(times(0)) * (times(1) * weight)
        right = sigmoid(times(2)) * (times(3) * weight)
        for j in range(2):
            left_f[pl.ds(p * 2 + j, C, stride=TILES), :] = left[:, j * 128 : j * 128 + 128]
            right_f[pl.ds(p * 2 + j, C, stride=TILES), :] = right[:, j * 128 : j * 128 + 128]
        gate[p] = sigmoid(times(4))

    def pack(u, part):
        def step(c, carry):
            at = pl.ds(pl.multiple_of(c * TILES + part * 8, 8), 8)
            both = jnp.concatenate([left_f[at, :], right_f[at, :]], axis=0)
            sides_s[u, part, c] = both.astype(jnp.bfloat16)
            return carry

        lax.fori_loop(0, C, step, 0, unroll=8)

    def send_sides(u, part, k):
        send_all(
            sides_s.at[u, part], sides_r.at[u, part], send_sem.at[u], recv_sem.at[u], k
        )

    def send_products(u):
        for k in range(2):
            send_all(
                prod_s.at[u], prod_r.at[u], send_sem.at[2 + u], recv_sem.at[2 + u], k
            )

    def first(p, carry):
        tiles = [
            jnp.concatenate([pair_ref[p * 2 + j], pair_ref[p * 2 + j + HALF]], axis=0)
            .astype(jnp.float32)
            .T
            for j in range(2)
        ]
        block = jnp.concatenate(tiles, axis=1)
        state[p] = block
        project(0, p, block)
        return carry

    lax.fori_loop(0, PAIRS // 2, first, 0, unroll=2)
    pack(0, 0)
    pl.semaphore_wait(pltpu.get_barrier_semaphore(), DEVICES - 1)
    send_sides(0, 0, 0)
    send_sides(0, 0, 1)
    lax.fori_loop(PAIRS // 2, PAIRS, first, 0, unroll=2)
    pack(0, 1)
    send_sides(0, 1, 0)
    send_sides(0, 1, 1)
    for n in (5, 6):
        loads[n].wait()
    turn_out(0)
    turn(1)
    turn_out(1)

    def swap(a, b):
        one = jnp.where(low, a, pltpu.roll(b, COLS, 1))
        two = jnp.where(low, pltpu.roll(a, COLS, 1), b)
        return one, two

    for u in range(2):
        whole = sides_r.at[u]
        pltpu.make_async_copy(whole, whole, recv_sem.at[u]).wait()

        def assemble(r, carry):
            at = pl.multiple_of(r * ROWS, ROWS)
            for m in range(4):
                tiles = [
                    [sides_r[u, part, r * 8 + 2 * m + j].astype(jnp.float32) for part in range(2)]
                    for j in range(2)
                ]
                for side, target in ((0, left_m), (8, right_m)):
                    turned = [
                        swap(tiles[0][part][side : side + 8], tiles[1][part][side : side + 8])
                        for part in range(2)
                    ]
                    for h in range(2):
                        both = jnp.concatenate([turned[0][h], turned[1][h]], axis=0)
                        target[pl.ds(at + 16 * h, 16), m * 128 : (m + 1) * 128] = both.astype(
                            jnp.bfloat16
                        )
            return carry

        lax.fori_loop(0, 16, assemble, 0, unroll=2)
        for q in range(4):
            if u == 0:
                dims = (((1,), (1,)), ((), ()))
                part = left_m[q * 128 : (q + 1) * 128, :]
            else:
                dims = (((0,), (0,)), ((), ()))
                part = left_m[:, q * 128 : (q + 1) * 128]
            product = lax.dot_general(part, right_m[...], dims, preferred_element_type=jnp.float32)
            for r in range(4):
                for m in range(4):
                    turned = [
                        swap(
                            product[r * 32 + e : r * 32 + e + 8, m * 128 : (m + 1) * 128],
                            product[r * 32 + 16 + e : r * 32 + 24 + e, m * 128 : (m + 1) * 128],
                        )
                        for e in (0, 8)
                    ]
                    for h in range(2):
                        both = jnp.concatenate([turned[0][h], turned[1][h]], axis=0)
                        prod_s[u, (q * 4 + r) * 8 + 2 * m + h] = both.astype(jnp.bfloat16)
        send_products(u)
        whole = prod_r.at[u]
        pltpu.make_async_copy(whole, whole, recv_sem.at[2 + u]).wait()

        def unpack(c, carry):
            left_f[pl.ds(pl.multiple_of(c * TILES, TILES), TILES), :] = prod_r[u, c].astype(jnp.float32)
            return carry

        lax.fori_loop(0, C, unpack, 0, unroll=8)

        def finish(p, carry):
            product = jnp.concatenate(
                [left_f[pl.ds(p * 2 + j, C, stride=TILES), :] for j in range(2)], axis=1
            )
            normout = normalise(product, wide(out_gain_t[u])).astype(jnp.bfloat16)
            update = jnp.dot(outw_t[u], normout, preferred_element_type=jnp.float32)
            new = (state[p] + gate[p] * update).astype(jnp.bfloat16).astype(jnp.float32)
            if u == 0:
                state[p] = new
            else:
                for j in range(2):
                    back = new[:, j * 128 : j * 128 + 128].T.astype(jnp.bfloat16)
                    out_ref[p * 2 + j] = back[0:COLS]
                    out_ref[p * 2 + j + HALF] = back[COLS : 2 * COLS]
            return carry

        if u == 0:

            def second(p, carry):
                project(1, p, state[p])
                return carry

            lax.fori_loop(0, PAIRS, finish, 0, unroll=4)
            for part in range(PARTS):
                lax.fori_loop(part * 4, part * 4 + 4, second, 0, unroll=2)
                pack(1, part)
                send_sides(1, part, 0)
                send_sides(1, part, 1)
        else:
            lax.fori_loop(0, PAIRS, finish, 0, unroll=4)

    for u in range(2):
        for part in range(PARTS):
            wait_bytes(sides_s.at[u, part], send_sem.at[u], DEVICES - 1)
        wait_bytes(prod_s.at[u], send_sem.at[2 + u], DEVICES - 1)


def shards(pair, residue_mask, in_gain, proj_weight, gate_weight, out_gain, out_weight):
    return pl.pallas_call(
        kernel,
        out_shape=jax.ShapeDtypeStruct(pair.shape, pair.dtype),
        in_specs=[pl.BlockSpec(memory_space=pl.ANY)] * 7,
        out_specs=pl.BlockSpec(memory_space=pltpu.VMEM),
        scratch_shapes=[
            pltpu.SMEM(residue_mask.shape, residue_mask.dtype),
            pltpu.VMEM(pair.shape, pair.dtype),
            pltpu.VMEM(in_gain.shape, in_gain.dtype),
            pltpu.VMEM(proj_weight.shape, proj_weight.dtype),
            pltpu.VMEM(gate_weight.shape, gate_weight.dtype),
            pltpu.VMEM(out_gain.shape, out_gain.dtype),
            pltpu.VMEM(out_weight.shape, out_weight.dtype),
            pltpu.VMEM((2, 640, 128), jnp.bfloat16),
            pltpu.VMEM((2, 128, 128), jnp.bfloat16),
            pltpu.VMEM((2, 128, 128), jnp.float32),
            pltpu.VMEM((2, 128, 128), jnp.float32),
            pltpu.VMEM((PAIRS, 8, 256), jnp.float32),
            pltpu.VMEM((PAIRS, 128, 256), jnp.float32),
            pltpu.VMEM((PAIRS, 128, 256), jnp.float32),
            pltpu.VMEM((C * TILES, 128), jnp.float32),
            pltpu.VMEM((C * TILES, 128), jnp.float32),
            pltpu.VMEM((2, PARTS, DEVICES, 16, 128), jnp.bfloat16),
            pltpu.VMEM((2, PARTS, DEVICES, 16, 128), jnp.bfloat16),
            pltpu.VMEM((2, DEVICES, 16, 128), jnp.bfloat16),
            pltpu.VMEM((2, DEVICES, 16, 128), jnp.bfloat16),
            pltpu.VMEM((512, 512), jnp.bfloat16),
            pltpu.VMEM((512, 512), jnp.bfloat16),
            pltpu.SemaphoreType.DMA((7,)),
            pltpu.SemaphoreType.DMA((4,)),
            pltpu.SemaphoreType.DMA((4,)),
        ],
        compiler_params=pltpu.CompilerParams(
            collective_id=0, has_side_effects=True, vmem_limit_bytes=48 * 1024 * 1024
        ),
    )(residue_mask, pair, in_gain, proj_weight, gate_weight, out_gain, out_weight)


def solution(mesh):
    placed = (P("row", "col", None), P(), P(), P(), P(), P(), P())
    return jax.shard_map(
        shards, mesh=mesh, in_specs=placed, out_specs=P("row", "col", None), check_vma=False
    )
```

time: 100 us -> 75 us (0.75)
  Pallas kernels: 93.4 us -> 68.2 us
    pallas_call x1, Pallas kernels: 93.4 us -> 68.2 us  [shards(): pl.pallas_call(kernel, out_shape=jax.ShapeDtypeStruct(pair.shape, pair.dt...]
where the time goes in v2:
time: 75 us; the launch traced here: 74.7 us
  Pallas kernels  68.2 us (91%)
  local copies, waits for them, and re-layouts  6.5 us (9%)
    pallas_call x1, Pallas kernels, shards(): pl.pallas_call(kernel, out_shape=jax.ShapeDtypeStruct(pair.shape, pair.dt...  68.2 us
    unnamed x15, local copies, waits for them, and re-layouts  6.5 us

profile of v2, /device:TPU:1, one launch (start us, length us, event | category | flops | bytes accessed | tf_op | source)
XLA Modules:
  0.0 74.7 jit_solution(5964840575269392221)
XLA Ops:
  0.0 0.0 copy-start
  0.0 1.0 %copy-done = bf16[32,64,128]{2,1,0:T(8,128)(2,1)S(1)} copy-done((bf16[32,64,128]{2,1,0:T(8,128)(2,1)S(1)}, bf16[32,64,128]{2,1,0:T(8,128)(2,1)}, u32[]{:S(2)}) %copy-start) | copy-done | bytes 524312
  1.0 0.0 copy-start.1
  1.0 0.9 %copy-done.1 = bf16[2,128,512]{2,1,0:T(8,128)(2,1)S(1)} copy-done((bf16[2,128,512]{2,1,0:T(8,128)(2,1)S(1)}, bf16[2,128,512]{2,1,0:T(8,128)(2,1)}, u32[]{:S(2)}) %copy-start.1) | copy-done | bytes 262168
  2.0 0.0 copy-start.2
  2.0 0.8 %copy-done.2 = bf16[2,128,128]{2,1,0:T(8,128)(2,1)S(1)} copy-done((bf16[2,128,128]{2,1,0:T(8,128)(2,1)S(1)}, bf16[2,128,128]{2,1,0:T(8,128)(2,1)}, u32[]{:S(2)}) %copy-start.2) | copy-done | bytes 65560
  2.8 0.0 copy-start.3
  2.8 0.8 %copy-done.3 = bf16[2,128,128]{2,1,0:T(8,128)(2,1)S(1)} copy-done((bf16[2,128,128]{2,1,0:T(8,128)(2,1)S(1)}, bf16[2,128,128]{2,1,0:T(8,128)(2,1)}, u32[]{:S(2)}) %copy-start.3) | copy-done | bytes 65560
  3.7 0.0 copy-start.4
  3.7 0.7 copy-done.4
  4.4 0.0 copy-start.5
  4.4 0.7 copy-done.5
  5.0 0.0 copy-start.6
  5.0 0.7 copy-done.6
  5.7 68.2 %shard_map.73 = bf16[32,64,128]{2,1,0:T(8,128)(2,1)S(1)} custom-call(s32[512]{0:T(512)S(1)} %copy-done.4, bf16[32,64,128]{2,1,0:T(8,128)(2,1)S(1)} %copy-done, f32[2,128]{1,0:T(2,128)S(1)} %copy-done.5, bf16[2,128,512]{2,1,0:T(8,128)(2,1)S(1)} %copy-done.1, bf16[2,128,128]{2,1,0:T(8,128)(2,1)S(1)} %copy-done.2, f32[2,128]{1,0:T(2,128)S(1)} %copy-done.6, ...), custom_call_target="tpu_custom_call" | custom-call | tf_op jit(solution)/shard_map/pallas_call | solution.py:366
  73.9 0.8 %copy.9 = bf16[32,64,128]{2,1,0:T(8,128)(2,1)} copy(bf16[32,64,128]{2,1,0:T(8,128)(2,1)S(1)} %shard_map.73) | data formatting | bytes 1048576
Async XLA Ops:
  0.0 1.0 %copy-start = (bf16[32,64,128]{2,1,0:T(8,128)(2,1)S(1)}, bf16[32,64,128]{2,1,0:T(8,128)(2,1)}, u32[]{:S(2)}) copy-start(bf16[32,64,128]{2,1,0:T(8,128)(2,1)} %pair_hbm.1) | copy-start | bytes 1572868
  1.0 0.9 %copy-start.1 = (bf16[2,128,512]{2,1,0:T(8,128)(2,1)S(1)}, bf16[2,128,512]{2,1,0:T(8,128)(2,1)}, u32[]{:S(2)}) copy-start(bf16[2,128,512]{2,1,0:T(8,128)(2,1)} %proj_hbm.1) | copy-start | bytes 786436
  2.0 0.8 %copy-start.2 = (bf16[2,128,128]{2,1,0:T(8,128)(2,1)S(1)}, bf16[2,128,128]{2,1,0:T(8,128)(2,1)}, u32[]{:S(2)}) copy-start(bf16[2,128,128]{2,1,0:T(8,128)(2,1)} %gate_hbm.1) | copy-start | bytes 196612
  2.8 0.8 %copy-start.3 = (bf16[2,128,128]{2,1,0:T(8,128)(2,1)S(1)}, bf16[2,128,128]{2,1,0:T(8,128)(2,1)}, u32[]{:S(2)}) copy-start(bf16[2,128,128]{2,1,0:T(8,128)(2,1)} %outw_hbm.1) | copy-start | bytes 196612
  3.7 0.7 copy-start.4
  4.4 0.7 copy-start.5
  5.0 0.7 copy-start.6

commit v3 on v2

--- a/solution.py
+++ b/solution.py
@@ -1,3 +1,5 @@
+import functools
+
 import jax
 import jax.numpy as jnp
 from jax import lax
@@ -31,17 +33,23 @@
     return lax.rem(a + 4, 4)
 
 
-def far_first(q):
-    return jnp.where(q == 0, 2, jnp.where(q == 3, 0, q * 2 - 1))
-
-
-def peer_at(s):
-    x, y, z, _ = coords()
-    a, b, c = lax.rem(s, 4), lax.rem(s // 4, 4), s // 16
-    dx = far_first(a)
-    dy = far_first(lax.rem(a + b, 4))
-    dz = far_first(lax.rem(a + b + c, 4))
-    return wrap(x + dx), wrap(y + dy), wrap(z + dz)
+def offsets():
+    far = (2, 1, 3, 0)
+    found = []
+    for s in range(DEVICES):
+        a, b, c, d = s % 4, s // 4 % 4, s // 16 % 4, 1 - s // 64
+        found.append((far[a], far[(a + b) % 4], far[(a + b + c) % 4], d))
+    found.remove((0, 0, 0, 0))
+    return found
+
+
+def peers():
+    x, y, z, k = coords()
+    rows = [[wrap(x + a) * 2 + (k if d == 0 else 1 - k) for a in range(4)] for d in range(2)]
+    cols = [wrap(y + a) * 2 for a in range(4)]
+    highs = [wrap(z + a) // 2 * 8 for a in range(4)]
+    lows = [lax.rem(wrap(z + a), 2) for a in range(4)]
+    return [(highs[c] + rows[d][a], cols[b] + lows[c]) for a, b, c, d in offsets()]
 
 
 def greet():
@@ -58,12 +66,9 @@
     lax.fori_loop(1, DEVICES, step, 0)
 
 
-def send_all(send, recv, send_sem, recv_sem, core):
-    _, _, _, k = coords()
+def send_all(others, send, recv, send_sem, recv_sem):
     me = lax.axis_index("row") * 8 + lax.axis_index("col")
-
-    def one(s):
-        row, col = device_at(*peer_at(s), core)
+    for row, col in others:
         pltpu.make_async_remote_copy(
             send.at[row * 8 + col],
             recv.at[me],
@@ -72,32 +77,7 @@
             device_id=(row, col),
             device_id_type=MESH,
         ).start()
-
-    def step(s, carry):
-        one(s)
-        return carry
-
-    lax.fori_loop(0, HERE, step, 0)
-    lax.fori_loop(HERE + 1, 64, step, 0)
-
-    @pl.when(k == core)
-    def _():
-        pltpu.make_async_copy(send.at[me], recv.at[me], recv_sem).start()
-
-    @pl.when(k != core)
-    def _():
-        one(HERE)
-
-
-def number_here():
-    for s in range(64):
-        a, b, c = s % 4, s // 4 % 4, s // 16
-        order = (2, 1, 3, 0)
-        if order[a] == order[(a + b) % 4] == order[(a + b + c) % 4] == 0:
-            return s
-
-
-HERE = number_here()
+    recv[me] = send[me]
 
 
 def wait_bytes(buffer, sem, count):
@@ -124,6 +104,7 @@
     gate_hbm,
     out_gain_hbm,
     outw_hbm,
+    out_hbm,
     out_ref,
     mask_ref,
     pair_ref,
@@ -145,15 +126,17 @@
     sides_r,
     prod_s,
     prod_r,
+    prod_f,
     left_m,
     right_m,
     in_sem,
+    out_sem,
     send_sem,
     recv_sem,
 ):
     row_index = lax.axis_index("row")
     col_index = lax.axis_index("col")
-    _, _, _, core = coords()
+    others = peers()
     loads = [
         pltpu.make_async_copy(source, target, in_sem.at[n])
         for n, (source, target) in enumerate(
@@ -167,6 +150,15 @@
                 (outw_hbm, outw_ref),
             )
         )
+    ]
+    stores = [
+        pltpu.make_async_copy(
+            out_ref.at[pl.ds(part * 8 + h * HALF, 8)],
+            out_hbm.at[pl.ds(part * 8 + h * HALF, 8)],
+            out_sem.at[part * 2 + h],
+        )
+        for part in range(PARTS)
+        for h in range(2)
     ]
     for load in loads:
         load.start()
@@ -228,16 +220,14 @@
 
         lax.fori_loop(0, C, step, 0, unroll=8)
 
-    def send_sides(u, part, k):
+    def send_sides(u, part):
         send_all(
-            sides_s.at[u, part], sides_r.at[u, part], send_sem.at[u], recv_sem.at[u], k
+            others,
+            sides_s.at[u, part],
+            sides_r.at[u, part],
+            send_sem.at[2 * u + part],
+            recv_sem.at[2 * u + part],
         )
-
-    def send_products(u):
-        for k in range(2):
-            send_all(
-                prod_s.at[u], prod_r.at[u], send_sem.at[2 + u], recv_sem.at[2 + u], k
-            )
 
     def first(p, carry):
         tiles = [
@@ -254,12 +244,10 @@
     lax.fori_loop(0, PAIRS // 2, first, 0, unroll=2)
     pack(0, 0)
     pl.semaphore_wait(pltpu.get_barrier_semaphore(), DEVICES - 1)
-    send_sides(0, 0, 0)
-    send_sides(0, 0, 1)
+    send_sides(0, 0)
     lax.fori_loop(PAIRS // 2, PAIRS, first, 0, unroll=2)
     pack(0, 1)
-    send_sides(0, 1, 0)
-    send_sides(0, 1, 1)
+    send_sides(0, 1)
     for n in (5, 6):
         loads[n].wait()
     turn_out(0)
@@ -272,62 +260,99 @@
         return one, two
 
     for u in range(2):
-        whole = sides_r.at[u]
-        pltpu.make_async_copy(whole, whole, recv_sem.at[u]).wait()
-
-        def assemble(r, carry):
-            at = pl.multiple_of(r * ROWS, ROWS)
+
+        def assemble(part, r, sides):
             for m in range(4):
                 tiles = [
-                    [sides_r[u, part, r * 8 + 2 * m + j].astype(jnp.float32) for part in range(2)]
-                    for j in range(2)
+                    sides_r[u, part, r * 8 + 2 * m + j].astype(jnp.float32) for j in range(2)
                 ]
-                for side, target in ((0, left_m), (8, right_m)):
-                    turned = [
-                        swap(tiles[0][part][side : side + 8], tiles[1][part][side : side + 8])
-                        for part in range(2)
+                for side, target in sides:
+                    both = jnp.concatenate(
+                        swap(tiles[0][side : side + 8], tiles[1][side : side + 8]), axis=0
+                    )
+                    at = pl.multiple_of(part * 256 + r * 16, 16)
+                    target[pl.ds(at, 16), m * 128 : (m + 1) * 128] = both.astype(jnp.bfloat16)
+
+        def assemble_natural(r):
+            for m in range(4):
+                turned = []
+                for part in range(PARTS):
+                    tiles = [
+                        sides_r[u, part, r * 8 + 2 * m + j].astype(jnp.float32) for j in range(2)
                     ]
-                    for h in range(2):
-                        both = jnp.concatenate([turned[0][h], turned[1][h]], axis=0)
-                        target[pl.ds(at + 16 * h, 16), m * 128 : (m + 1) * 128] = both.astype(
-                            jnp.bfloat16
-                        )
-            return carry
-
-        lax.fori_loop(0, 16, assemble, 0, unroll=2)
+                    turned.append(swap(tiles[0][8:16], tiles[1][8:16]))
+                for h in range(2):
+                    both = jnp.concatenate([turned[0][h], turned[1][h]], axis=0)
+                    at = pl.multiple_of(r * ROWS + 16 * h, 16)
+                    right_m[pl.ds(at, 16), m * 128 : (m + 1) * 128] = both.astype(jnp.bfloat16)
+
+        def left_only(part, r):
+            assemble(part, r, ((0, left_m),))
+
+        def both_sides(part, r):
+            assemble(part, r, ((0, left_m), (8, right_m)))
+
+        def every(body):
+            def step(r, carry):
+                body(r)
+                return carry
+
+            lax.fori_loop(0, 16, step, 0, unroll=4)
+
+        for part in range(PARTS):
+            wait_bytes(sides_r.at[u, part], recv_sem.at[2 * u + part], DEVICES - 1)
+            every(functools.partial(left_only if u == 0 else both_sides, part))
+        if u == 0:
+            every(assemble_natural)
+
+        def deliver(upper, lower, r, m):
+            turned = [swap(upper[e], lower[e]) for e in range(2)]
+            for h in range(2):
+                both = jnp.concatenate([turned[0][h], turned[1][h]], axis=0)
+                prod_s[u, r * 8 + 2 * m + h] = both.astype(jnp.bfloat16)
+
         for q in range(4):
             if u == 0:
-                dims = (((1,), (1,)), ((), ()))
-                part = left_m[q * 128 : (q + 1) * 128, :]
+                rows = jnp.concatenate(
+                    [left_m[part * 256 + q * 64 : part * 256 + q * 64 + 64, :] for part in range(2)],
+                    axis=0,
+                )
+                product = lax.dot_general(
+                    rows,
+                    right_m[...],
+                    (((1,), (1,)), ((), ())),
+                    preferred_element_type=jnp.float32,
+                )
             else:
-                dims = (((0,), (0,)), ((), ()))
-                part = left_m[:, q * 128 : (q + 1) * 128]
-            product = lax.dot_general(part, right_m[...], dims, preferred_element_type=jnp.float32)
+                product = lax.dot_general(
+                    left_m[:, q * 128 : (q + 1) * 128],
+                    right_m[...],
+                    (((0,), (0,)), ((), ())),
+                    preferred_element_type=jnp.float32,
+                )
             for r in range(4):
                 for m in range(4):
-                    turned = [
-                        swap(
-                            product[r * 32 + e : r * 32 + e + 8, m * 128 : (m + 1) * 128],
-                            product[r * 32 + 16 + e : r * 32 + 24 + e, m * 128 : (m + 1) * 128],
-                        )
-                        for e in (0, 8)
-                    ]
-                    for h in range(2):
-                        both = jnp.concatenate([turned[0][h], turned[1][h]], axis=0)
-                        prod_s[u, (q * 4 + r) * 8 + 2 * m + h] = both.astype(jnp.bfloat16)
-        send_products(u)
-        whole = prod_r.at[u]
-        pltpu.make_async_copy(whole, whole, recv_sem.at[2 + u]).wait()
+                    across = slice(m * 128, (m + 1) * 128)
+                    if u == 0:
+                        starts = [[e * 64 + r * 16 + h * 8 for e in range(2)] for h in range(2)]
+                    else:
+                        starts = [[r * 32 + h * 16 + e * 8 for e in range(2)] for h in range(2)]
+                    upper, lower = (
+                        [product[at : at + 8, across] for at in starts[h]] for h in range(2)
+                    )
+                    deliver(upper, lower, q * 4 + r, m)
+        send_all(others, prod_s.at[u], prod_r.at[u], send_sem.at[4 + u], recv_sem.at[4 + u])
+        wait_bytes(prod_r.at[u], recv_sem.at[4 + u], DEVICES - 1)
 
         def unpack(c, carry):
-            left_f[pl.ds(pl.multiple_of(c * TILES, TILES), TILES), :] = prod_r[u, c].astype(jnp.float32)
+            prod_f[pl.ds(pl.multiple_of(c * TILES, TILES), TILES), :] = prod_r[u, c].astype(jnp.float32)
             return carry
 
         lax.fori_loop(0, C, unpack, 0, unroll=8)
 
         def finish(p, carry):
             product = jnp.concatenate(
-                [left_f[pl.ds(p * 2 + j, C, stride=TILES), :] for j in range(2)], axis=1
+                [prod_f[pl.ds(p * 2 + j, C, stride=TILES), :] for j in range(2)], axis=1
             )
             normout = normalise(product, wide(out_gain_t[u])).astype(jnp.bfloat16)
             update = jnp.dot(outw_t[u], normout, preferred_element_type=jnp.float32)
@@ -341,25 +366,26 @@
                     out_ref[p * 2 + j + HALF] = back[COLS : 2 * COLS]
             return carry
 
-        if u == 0:
-
-            def second(p, carry):
-                project(1, p, state[p])
-                return carry
-
-            lax.fori_loop(0, PAIRS, finish, 0, unroll=4)
-            for part in range(PARTS):
+        def second(p, carry):
+            project(1, p, state[p])
+            return carry
+
+        for part in range(PARTS):
+            lax.fori_loop(part * 4, part * 4 + 4, finish, 0, unroll=4)
+            if u == 0:
                 lax.fori_loop(part * 4, part * 4 + 4, second, 0, unroll=2)
                 pack(1, part)
-                send_sides(1, part, 0)
-                send_sides(1, part, 1)
-        else:
-            lax.fori_loop(0, PAIRS, finish, 0, unroll=4)
+                send_sides(1, part)
+            else:
+                for h in range(2):
+                    stores[part * 2 + h].start()
 
     for u in range(2):
         for part in range(PARTS):
-            wait_bytes(sides_s.at[u, part], send_sem.at[u], DEVICES - 1)
-        wait_bytes(prod_s.at[u], send_sem.at[2 + u], DEVICES - 1)
+            wait_bytes(sides_s.at[u, part], send_sem.at[2 * u + part], DEVICES - 1)
+        wait_bytes(prod_s.at[u], send_sem.at[4 + u], DEVICES - 1)
+    for store in stores:
+        store.wait()
 
 
 def shards(pair, residue_mask, in_gain, proj_weight, gate_weight, out_gain, out_weight):
@@ -367,8 +393,9 @@
         kernel,
         out_shape=jax.ShapeDtypeStruct(pair.shape, pair.dtype),
         in_specs=[pl.BlockSpec(memory_space=pl.ANY)] * 7,
-        out_specs=pl.BlockSpec(memory_space=pltpu.VMEM),
+        out_specs=pl.BlockSpec(memory_space=pl.ANY),
         scratch_shapes=[
+            pltpu.VMEM(pair.shape, pair.dtype),
             pltpu.SMEM(residue_mask.shape, residue_mask.dtype),
             pltpu.VMEM(pair.shape, pair.dtype),
             pltpu.VMEM(in_gain.shape, in_gain.dtype),
@@ -389,14 +416,16 @@
             pltpu.VMEM((2, PARTS, DEVICES, 16, 128), jnp.bfloat16),
             pltpu.VMEM((2, DEVICES, 16, 128), jnp.bfloat16),
             pltpu.VMEM((2, DEVICES, 16, 128), jnp.bfloat16),
+            pltpu.VMEM((C * TILES, 128), jnp.float32),
             pltpu.VMEM((512, 512), jnp.bfloat16),
             pltpu.VMEM((512, 512), jnp.bfloat16),
             pltpu.SemaphoreType.DMA((7,)),
             pltpu.SemaphoreType.DMA((4,)),
-            pltpu.SemaphoreType.DMA((4,)),
+            pltpu.SemaphoreType.DMA((6,)),
+            pltpu.SemaphoreType.DMA((6,)),
         ],
         compiler_params=pltpu.CompilerParams(
-            collective_id=0, has_side_effects=True, vmem_limit_bytes=48 * 1024 * 1024
+            collective_id=0, has_side_effects=True, vmem_limit_bytes=58 * 1024 * 1024
         ),
     )(residue_mask, pair, in_gain, proj_weight, gate_weight, out_gain, out_weight)
 

time: 75 us -> 67.3 us (0.90)
  local copies, waits for them, and re-layouts: 6.5 us -> 1.87 us
  Pallas kernels: 68.2 us -> 64.8 us
    unnamed x15 -> x1, local copies, waits for them, and re-layouts: 6.5 us -> 1.87 us
    pallas_call x1, Pallas kernels: 68.2 us -> 64.8 us  [shards(): pl.pallas_call(kernel, out_shape=jax.ShapeDtypeStruct(pair.shape, pair.dt...]
where the time goes in v3:
time: 67.3 us; the launch traced here: 66.7 us
  Pallas kernels  64.8 us (96%)
  local copies, waits for them, and re-layouts  1.87 us (3%)
    pallas_call x1, Pallas kernels, shards(): pl.pallas_call(kernel, out_shape=jax.ShapeDtypeStruct(pair.shape, pair.dt...  64.8 us
    unnamed x1, local copies, waits for them, and re-layouts  1.87 us

profile of v3, /device:TPU:1, one launch (start us, length us, event | category | flops | bytes accessed | tf_op | source)
XLA Modules:
  0.0 66.7 jit_solution(18206263904862134292)
XLA Ops:
  0.0 64.8 %shard_map.73 = bf16[32,64,128]{2,1,0:T(8,128)(2,1)} custom-call(s32[512]{0:T(512)} %mask_hbm.1, bf16[32,64,128]{2,1,0:T(8,128)(2,1)} %pair_hbm.1, f32[2,128]{1,0:T(2,128)} %in_gain_hbm.1, bf16[2,128,512]{2,1,0:T(8,128)(2,1)} %proj_hbm.1, bf16[2,128,128]{2,1,0:T(8,128)(2,1)} %gate_hbm.1, f32[2,128]{1,0:T(2,128)} %out_gain_hbm.1, bf16[2,128,128]{2,1,0:T(8,128)(2,1)} %outw_hbm.1), custom_call_target="tpu_custom_call" | custom-call | tf_op jit(solution)/shard_map/pallas_call | solution.py:392
  64.8 1.9 %copy.9 = bf16[32,64,128]{2,1,0:T(8,128)(2,1)} copy(bf16[32,64,128]{2,1,0:T(8,128)(2,1)} %shard_map.73) | data formatting | bytes 1048576

commit v4 on v3

--- a/solution.py
+++ b/solution.py
@@ -52,18 +52,15 @@
     return [(highs[c] + rows[d][a], cols[b] + lows[c]) for a, b, c, d in offsets()]
 
 
-def greet():
+def greet(others):
     barrier = pltpu.get_barrier_semaphore()
-    me = lax.axis_index("row") * 8 + lax.axis_index("col")
-
-    def step(s, carry):
-        peer = lax.rem(me + s, DEVICES)
-        pl.semaphore_signal(
-            barrier, inc=1, device_id=(peer // 8, lax.rem(peer, 8)), device_id_type=MESH
-        )
-        return carry
-
-    lax.fori_loop(1, DEVICES, step, 0)
+    for peer in sorted_far(others):
+        pl.semaphore_signal(barrier, inc=1, device_id=peer, device_id_type=MESH)
+
+
+def sorted_far(others):
+    far = [sum((0, 1, 2, 1)[v] for v in offset[:3]) for offset in offsets()]
+    return [others[n] for n in sorted(range(DEVICES - 1), key=lambda n: -far[n])]
 
 
 def send_all(others, send, recv, send_sem, recv_sem):
@@ -162,7 +159,7 @@
     ]
     for load in loads:
         load.start()
-    greet()
+    greet(others)
 
     def turn(u):
         for n in range(4):

time: 67.3 us -> 65.8 us (0.978)
  Pallas kernels: 64.8 us -> 63.3 us
    pallas_call x1, Pallas kernels: 64.8 us -> 63.3 us  [shards(): pl.pallas_call(kernel, out_shape=jax.ShapeDtypeStruct(pair.shape, pair.dt...]
where the time goes in v4:
time: 65.8 us; the launch traced here: 65.2 us
  Pallas kernels  63.3 us (96%)
  local copies, waits for them, and re-layouts  1.87 us (3%)
    pallas_call x1, Pallas kernels, shards(): pl.pallas_call(kernel, out_shape=jax.ShapeDtypeStruct(pair.shape, pair.dt...  63.3 us
    unnamed x1, local copies, waits for them, and re-layouts  1.87 us

profile of v4, /device:TPU:1, one launch (start us, length us, event | category | flops | bytes accessed | tf_op | source)
XLA Modules:
  0.0 65.2 jit_solution(10081107344611746379)
XLA Ops:
  0.0 63.3 %shard_map.73 = bf16[32,64,128]{2,1,0:T(8,128)(2,1)} custom-call(s32[512]{0:T(512)} %mask_hbm.1, bf16[32,64,128]{2,1,0:T(8,128)(2,1)} %pair_hbm.1, f32[2,128]{1,0:T(2,128)} %in_gain_hbm.1, bf16[2,128,512]{2,1,0:T(8,128)(2,1)} %proj_hbm.1, bf16[2,128,128]{2,1,0:T(8,128)(2,1)} %gate_hbm.1, f32[2,128]{1,0:T(2,128)} %out_gain_hbm.1, bf16[2,128,128]{2,1,0:T(8,128)(2,1)} %outw_hbm.1), custom_call_target="tpu_custom_call" | custom-call | tf_op jit(solution)/shard_map/pallas_call | solution.py:389
  63.4 1.9 %copy.9 = bf16[32,64,128]{2,1,0:T(8,128)(2,1)} copy(bf16[32,64,128]{2,1,0:T(8,128)(2,1)} %shard_map.73) | data formatting | bytes 1048576

commit v5 on v3

v5 whole, which is shorter than its diff:
```python
import jax
import jax.numpy as jnp
from jax import lax
from jax.experimental import pallas as pl
from jax.experimental.pallas import tpu as pltpu
from jax.sharding import PartitionSpec as P

EPSILON = 1e-05
MESH = pl.DeviceIdType.MESH
CHIPS = 64
C = 128
ROWS = 32
COLS = 64
HALF = ROWS // 2
TILES = 16
PAIRS = 8
PARTS = 2


def coords():
    r = lax.axis_index("row")
    c = lax.axis_index("col")
    return lax.rem(r // 2, 4), c // 2, (r // 8) * 2 + lax.rem(c, 2), lax.rem(r, 2)


def device_at(x, y, z, k):
    return ((z // 2) * 8 + x * 2 + k, y * 2 + lax.rem(z, 2))


def wrap(a):
    return lax.rem(a + 4, 4)


def offsets():
    far = (2, 1, 3, 0)
    found = []
    for s in range(CHIPS):
        a, b, c = s % 4, s // 4 % 4, s // 16
        found.append((far[a], far[(a + b) % 4], far[(a + b + c) % 4]))
    found.remove((0, 0, 0))
    return found


def peers():
    x, y, z, _ = coords()
    rows = [wrap(x + a) for a in range(4)]
    cols = [wrap(y + a) * 2 for a in range(4)]
    highs = [wrap(z + a) // 2 * 4 for a in range(4)]
    lows = [lax.rem(wrap(z + a), 2) for a in range(4)]
    return [(highs[c] + rows[a], cols[b] + lows[c]) for a, b, c in offsets()]


def greet(others, core, sibling):
    barrier = pltpu.get_barrier_semaphore()
    far = [sum((0, 1, 2, 1)[v] for v in offset) for offset in offsets()]
    for n in sorted(range(CHIPS - 1), key=lambda n: -far[n]):
        row, col = others[n]
        pl.semaphore_signal(
            barrier, inc=1, device_id=(row * 2 + core, col), device_id_type=MESH
        )
    pl.semaphore_signal(barrier, inc=1, device_id=sibling, device_id_type=MESH)


def wait_bytes(buffer, sem, count):
    part = buffer.at[pl.ds(0, count)]
    pltpu.make_async_copy(part, part, sem).wait()


def sigmoid(v):
    return 0.5 * jnp.tanh(0.5 * v) + 0.5


def normalise(values, gain):
    center = jnp.mean(values, axis=0, keepdims=True)
    moved = values - center
    spread = jnp.mean(moved * moved, axis=0, keepdims=True)
    return moved * lax.rsqrt(spread + EPSILON) * gain


def kernel(
    mask_hbm,
    pair_hbm,
    in_gain_hbm,
    proj_hbm,
    gate_hbm,
    out_gain_hbm,
    outw_hbm,
    out_hbm,
    out_ref,
    mask_ref,
    pair_ref,
    in_gain_ref,
    proj_ref,
    gate_ref,
    out_gain_ref,
    outw_ref,
    proj_t,
    outw_t,
    in_gain_t,
    out_gain_t,
    weight_of,
    state,
    gate,
    left_f,
    right_f,
    sides_s,
    sides_r,
    prod_s,
    prod_r,
    prod_f,
    left_m,
    left_k,
    right_m,
    in_sem,
    out_sem,
    over_send,
    over_recv,
    send_sem,
    recv_sem,
):
    row_index = lax.axis_index("row")
    col_index = lax.axis_index("col")
    core = lax.rem(row_index, 2)
    half_row = row_index // 2
    chip = half_row * 8 + col_index
    sibling = (half_row * 2 + 1 - core, col_index)
    others = peers()
    loads = [
        pltpu.make_async_copy(source, target, in_sem.at[n])
        for n, (source, target) in enumerate(
            (
                (mask_hbm, mask_ref),
                (proj_hbm, proj_ref),
                (gate_hbm, gate_ref),
                (in_gain_hbm, in_gain_ref),
                (pair_hbm, pair_ref),
                (out_gain_hbm, out_gain_ref),
                (outw_hbm, outw_ref),
            )
        )
    ]
    stores = [
        pltpu.make_async_copy(
            out_ref.at[pl.ds(part * 8 + h * HALF, 8)],
            out_hbm.at[pl.ds(part * 8 + h * HALF, 8)],
            out_sem.at[part * 2 + h],
        )
        for part in range(PARTS)
        for h in range(2)
    ]
    for load in loads:
        load.start()
    greet(others, core, sibling)

    def turn(u):
        for n in range(4):
            block = proj_ref[u, :, n * 128 : (n + 1) * 128].astype(jnp.float32)
            proj_t[u, n * 128 : (n + 1) * 128, :] = block.T.astype(jnp.bfloat16)
        proj_t[u, 512:640, :] = gate_ref[u].astype(jnp.float32).T.astype(jnp.bfloat16)
        in_gain_t[u] = jnp.broadcast_to(in_gain_ref[u : u + 1, :], (128, 128)).T

    def turn_out(u):
        outw_t[u] = outw_ref[u].astype(jnp.float32).T.astype(jnp.bfloat16)
        out_gain_t[u] = jnp.broadcast_to(out_gain_ref[u : u + 1, :], (128, 128)).T

    loads[0].wait()
    lane = lax.broadcasted_iota(jnp.int32, (8, 128), 1)
    low = lane < COLS
    lane_col = lax.rem(lane, COLS)
    col_flags = jnp.zeros((8, 128), jnp.float32)
    for j in range(COLS):
        flag = mask_ref[col_index * COLS + j].astype(jnp.float32)
        col_flags = jnp.where(lane_col == j, flag, col_flags)
    for t in range(TILES):
        upper = mask_ref[row_index * ROWS + t].astype(jnp.float32)
        lower = mask_ref[row_index * ROWS + HALF + t].astype(jnp.float32)
        weight_of[t // 2, :, t % 2 * 128 : t % 2 * 128 + 128] = col_flags * jnp.where(low, upper, lower)
    for n in (1, 2, 3):
        loads[n].wait()
    turn(0)
    loads[4].wait()

    def wide(column):
        return jnp.concatenate([column, column], axis=1)

    def project(u, p, values):
        normed = normalise(values, wide(in_gain_t[u])).astype(jnp.bfloat16)
        weight = weight_of[p][0:1, :]

        def times(n):
            return jnp.dot(
                proj_t[u, n * 128 : (n + 1) * 128, :], normed, preferred_element_type=jnp.float32
            )

        left = sigmoid(times(0)) * (times(1) * weight)
        right = sigmoid(times(2)) * (times(3) * weight)
        for j in range(2):
            left_f[pl.ds(p * 2 + j, C, stride=TILES), :] = left[:, j * 128 : j * 128 + 128]
            right_f[pl.ds(p * 2 + j, C, stride=TILES), :] = right[:, j * 128 : j * 128 + 128]
        gate[p] = sigmoid(times(4))

    def pack(u, part):
        def step(c, carry):
            at = pl.ds(pl.multiple_of(c * TILES + part * 8, 8), 8)
            both = jnp.concatenate([left_f[at, :], right_f[at, :]], axis=0)
            sides_s[u, part, c] = both.astype(jnp.bfloat16)
            return carry

        lax.fori_loop(0, C, step, 0, unroll=8)

    def channel(row, col, g):
        return (row * 2 + g) * 8 + col

    def send_sides(u, g, part):
        sem = (u * 2 + g) * 2 + part
        for row, col in others:
            pltpu.make_async_remote_copy(
                sides_s.at[u, part, channel(row, col, g)],
                sides_r.at[u, g, part, chip],
                send_sem.at[sem],
                recv_sem.at[sem],
                device_id=(row * 2 + core, col),
                device_id_type=MESH,
            ).start()
        sides_r[u, g, part, chip] = sides_s[u, part, channel(half_row, col_index, g)]

    def send_products(u, g):
        sem = 8 + u * 2 + g
        own = channel(half_row, col_index, g)
        for row, col in others:
            pltpu.make_async_remote_copy(
                prod_s.at[u, g, row * 8 + col],
                prod_r.at[u, own],
                send_sem.at[sem],
                recv_sem.at[sem],
                device_id=(row * 2 + core, col),
                device_id_type=MESH,
            ).start()
        prod_r[u, own] = prod_s[u, g, chip]

    def hand_over(buffer, sem):
        pltpu.make_async_remote_copy(
            buffer,
            buffer,
            over_send.at[sem],
            over_recv.at[sem],
            device_id=sibling,
            device_id_type=MESH,
        ).start()

    def first(p, carry):
        tiles = [
            jnp.concatenate([pair_ref[p * 2 + j], pair_ref[p * 2 + j + HALF]], axis=0)
            .astype(jnp.float32)
            .T
            for j in range(2)
        ]
        block = jnp.concatenate(tiles, axis=1)
        state[p] = block
        project(0, p, block)
        return carry

    lax.fori_loop(0, PAIRS // 2, first, 0, unroll=4)
    pack(0, 0)
    pl.semaphore_wait(pltpu.get_barrier_semaphore(), CHIPS)
    send_sides(0, 0, 0)
    lax.fori_loop(PAIRS // 2, PAIRS, first, 0, unroll=4)
    pack(0, 1)
    send_sides(0, 0, 1)
    send_sides(0, 1, 0)
    send_sides(0, 1, 1)
    for n in (5, 6):
        loads[n].wait()
    turn_out(0)
    turn(1)
    turn_out(1)

    def swap(a, b):
        one = jnp.where(low, a, pltpu.roll(b, COLS, 1))
        two = jnp.where(low, pltpu.roll(a, COLS, 1), b)
        return one, two

    def every(body):
        def step(q, carry):
            body(q)
            return carry

        lax.fori_loop(0, 8, step, 0, unroll=8)

    def turned_sides(u, g, part, q, m, side):
        tiles = [
            sides_r[u, g, part, q * 8 + 2 * m + j][side : side + 8, :].astype(jnp.float32)
            for j in range(2)
        ]
        return swap(tiles[0], tiles[1])

    for u in range(2):
        for g in range(2):
            for part in range(PARTS):
                wait_bytes(
                    sides_r.at[u, g, part], recv_sem.at[(u * 2 + g) * 2 + part], CHIPS - 1
                )

                def assemble(q):
                    for m in range(4):
                        across = slice(m * 128, (m + 1) * 128)
                        both = jnp.concatenate(turned_sides(u, g, part, q, m, 0), axis=0)
                        if u == 0:
                            at = pl.multiple_of(part * 128 + q * 16, 16)
                            left_m[g, pl.ds(at, 16), across] = both.astype(jnp.bfloat16)
                        else:
                            at = pl.multiple_of(part * 256 + core * 128 + q * 16, 16)
                            left_k[g, pl.ds(at, 16), across] = both.astype(jnp.bfloat16)
                            both = jnp.concatenate(turned_sides(u, g, part, q, m, 8), axis=0)
                            right_m[1, g, pl.ds(at, 16), across] = both.astype(jnp.bfloat16)

                every(assemble)
                if u == 1:
                    rows = pl.ds(pl.multiple_of(part * 256 + core * 128, 128), 128)
                    hand_over(left_k.at[g, rows], 2 + g * 4 + part * 2)
                    hand_over(right_m.at[1, g, rows], 3 + g * 4 + part * 2)
            if u == 0:

                def assemble_natural(q):
                    for m in range(4):
                        turned = [turned_sides(0, g, part, q, m, 8) for part in range(PARTS)]
                        for h in range(2):
                            both = jnp.concatenate([turned[0][h], turned[1][h]], axis=0)
                            at = pl.multiple_of((q * 2 + core) * ROWS + 16 * h, 16)
                            right_m[0, g, pl.ds(at, 16), m * 128 : (m + 1) * 128] = both.astype(
                                jnp.bfloat16
                            )

                every(assemble_natural)
                for q in range(8):
                    at = pl.multiple_of((q * 2 + core) * ROWS, ROWS)
                    hand_over(right_m.at[0, g, pl.ds(at, ROWS)], g)
                wait_bytes(right_m.at[0, g], over_recv.at[g], 256)
            else:
                for n in range(4):
                    wait_bytes(right_m.at[1, g], over_recv.at[2 + g * 4 + n], 128)

            def deliver(upper, lower, q, m):
                turned = [swap(upper[e], lower[e]) for e in range(2)]
                for h in range(2):
                    both = jnp.concatenate([turned[0][h], turned[1][h]], axis=0)
                    prod_s[u, g, q * 8 + 2 * m + h] = both.astype(jnp.bfloat16)

            if u == 0:
                for n in range(2):
                    rows = jnp.concatenate(
                        [
                            left_m[g, part * 128 + n * 64 : part * 128 + n * 64 + 64, :]
                            for part in range(2)
                        ],
                        axis=0,
                    )
                    product = lax.dot_general(
                        rows,
                        right_m[0, g],
                        (((1,), (1,)), ((), ())),
                        preferred_element_type=jnp.float32,
                    )
                    for q in range(4):
                        for m in range(4):
                            across = slice(m * 128, (m + 1) * 128)
                            upper, lower = (
                                [
                                    product[e * 64 + q * 16 + h * 8 :, across][:8]
                                    for e in range(2)
                                ]
                                for h in range(2)
                            )
                            deliver(upper, lower, n * 4 + q, m)
            else:
                first_core = core == 0
                for n in range(4):
                    product = lax.dot_general(
                        left_k[g, :, n * 128 : (n + 1) * 128],
                        right_m[1, g],
                        (((0,), (0,)), ((), ())),
                        preferred_element_type=jnp.float32,
                    )
                    for q in range(2):
                        for m in range(4):
                            across = slice(m * 128, (m + 1) * 128)
                            upper, lower = (
                                [
                                    jnp.where(
                                        first_core,
                                        product[q * 64 + h * 16 + e * 8 :, across][:8],
                                        product[q * 64 + 32 + h * 16 + e * 8 :, across][:8],
                                    )
                                    for e in range(2)
                                ]
                                for h in range(2)
                            )
                            deliver(upper, lower, n * 2 + q, m)
            send_products(u, g)

        for g in range(2):
            wait_bytes(prod_r.at[u], recv_sem.at[8 + u * 2 + g], CHIPS - 1)

            def unpack(q, carry):
                for col in range(8):
                    c = (q * 2 + g) * 8 + col
                    prod_f[pl.ds(pl.multiple_of(c * TILES, TILES), TILES), :] = prod_r[u, c].astype(
                        jnp.float32
                    )
                return carry

            lax.fori_loop(0, 8, unpack, 0)

        def finish(p, carry):
            product = jnp.concatenate(
                [prod_f[pl.ds(p * 2 + j, C, stride=TILES), :] for j in range(2)], axis=1
            )
            normout = normalise(product, wide(out_gain_t[u])).astype(jnp.bfloat16)
            update = jnp.dot(outw_t[u], normout, preferred_element_type=jnp.float32)
            new = (state[p] + gate[p] * update).astype(jnp.bfloat16).astype(jnp.float32)
            if u == 0:
                state[p] = new
            else:
                for j in range(2):
                    back = new[:, j * 128 : j * 128 + 128].T.astype(jnp.bfloat16)
                    out_ref[p * 2 + j] = back[0:COLS]
                    out_ref[p * 2 + j + HALF] = back[COLS : 2 * COLS]
            return carry

        def second(p, carry):
            project(1, p, state[p])
            return carry

        for part in range(PARTS):
            lax.fori_loop(part * 4, part * 4 + 4, finish, 0, unroll=4)
            if u == 0:
                lax.fori_loop(part * 4, part * 4 + 4, second, 0, unroll=4)
                pack(1, part)
                send_sides(1, 0, part)
            else:
                for h in range(2):
                    stores[part * 2 + h].start()
        if u == 0:
            for part in range(PARTS):
                send_sides(1, 1, part)

    for u in range(2):
        for g in range(2):
            for part in range(PARTS):
                sem = (u * 2 + g) * 2 + part
                wait_bytes(sides_r.at[u, g, part], send_sem.at[sem], CHIPS - 1)
            wait_bytes(prod_s.at[u, g], send_sem.at[8 + u * 2 + g], CHIPS - 1)
    for g in range(2):
        wait_bytes(right_m.at[0, g], over_send.at[g], 256)
        for n in range(4):
            wait_bytes(right_m.at[1, g], over_send.at[2 + g * 4 + n], 128)
    for store in stores:
        store.wait()


def shards(pair, residue_mask, in_gain, proj_weight, gate_weight, out_gain, out_weight):
    return pl.pallas_call(
        kernel,
        out_shape=jax.ShapeDtypeStruct(pair.shape, pair.dtype),
        in_specs=[pl.BlockSpec(memory_space=pl.ANY)] * 7,
        out_specs=pl.BlockSpec(memory_space=pl.ANY),
        scratch_shapes=[
            pltpu.VMEM(pair.shape, pair.dtype),
            pltpu.SMEM(residue_mask.shape, residue_mask.dtype),
            pltpu.VMEM(pair.shape, pair.dtype),
            pltpu.VMEM(in_gain.shape, in_gain.dtype),
            pltpu.VMEM(proj_weight.shape, proj_weight.dtype),
            pltpu.VMEM(gate_weight.shape, gate_weight.dtype),
            pltpu.VMEM(out_gain.shape, out_gain.dtype),
            pltpu.VMEM(out_weight.shape, out_weight.dtype),
            pltpu.VMEM((2, 640, 128), jnp.bfloat16),
            pltpu.VMEM((2, 128, 128), jnp.bfloat16),
            pltpu.VMEM((2, 128, 128), jnp.float32),
            pltpu.VMEM((2, 128, 128), jnp.float32),
            pltpu.VMEM((PAIRS, 8, 256), jnp.float32),
            pltpu.VMEM((PAIRS, 128, 256), jnp.float32),
            pltpu.VMEM((PAIRS, 128, 256), jnp.float32),
            pltpu.VMEM((C * TILES, 128), jnp.float32),
            pltpu.VMEM((C * TILES, 128), jnp.float32),
            pltpu.VMEM((2, PARTS, C, 16, 128), jnp.bfloat16),
            pltpu.VMEM((2, 2, PARTS, CHIPS, 16, 128), jnp.bfloat16),
            pltpu.VMEM((2, 2, CHIPS, 16, 128), jnp.bfloat16),
            pltpu.VMEM((2, C, 16, 128), jnp.bfloat16),
            pltpu.VMEM((C * TILES, 128), jnp.float32),
            pltpu.VMEM((2, 256, 512), jnp.bfloat16),
            pltpu.VMEM((2, 512, 512), jnp.bfloat16),
            pltpu.VMEM((2, 2, 512, 512), jnp.bfloat16),
            pltpu.SemaphoreType.DMA((7,)),
            pltpu.SemaphoreType.DMA((4,)),
            pltpu.SemaphoreType.DMA((10,)),
            pltpu.SemaphoreType.DMA((10,)),
            pltpu.SemaphoreType.DMA((12,)),
            pltpu.SemaphoreType.DMA((12,)),
        ],
        compiler_params=pltpu.CompilerParams(
            collective_id=0, has_side_effects=True, vmem_limit_bytes=58 * 1024 * 1024
        ),
    )(residue_mask, pair, in_gain, proj_weight, gate_weight, out_gain, out_weight)


def solution(mesh):
    placed = (P("row", "col", None), P(), P(), P(), P(), P(), P())
    return jax.shard_map(
        shards, mesh=mesh, in_specs=placed, out_specs=P("row", "col", None), check_vma=False
    )
```

time: 67.3 us -> 63.6 us (0.945)
  Pallas kernels: 64.8 us -> 61.5 us
    pallas_call x1, Pallas kernels: 64.8 us -> 61.5 us  [shards(): pl.pallas_call(kernel, out_shape=jax.ShapeDtypeStruct(pair.shape, pair.dt...]
where the time goes in v5:
time: 63.6 us; the launch traced here: 63.4 us
  Pallas kernels  61.5 us (97%)
  local copies, waits for them, and re-layouts  1.87 us (3%)
    pallas_call x1, Pallas kernels, shards(): pl.pallas_call(kernel, out_shape=jax.ShapeDtypeStruct(pair.shape, pair.dt...  61.5 us
    unnamed x1, local copies, waits for them, and re-layouts  1.87 us

profile of v5, /device:TPU:1, one launch (start us, length us, event | category | flops | bytes accessed | tf_op | source)
XLA Modules:
  0.0 63.4 jit_solution(213572224105681656)
XLA Ops:
  0.0 61.5 %shard_map.73 = bf16[32,64,128]{2,1,0:T(8,128)(2,1)} custom-call(s32[512]{0:T(512)} %mask_hbm.1, bf16[32,64,128]{2,1,0:T(8,128)(2,1)} %pair_hbm.1, f32[2,128]{1,0:T(2,128)} %in_gain_hbm.1, bf16[2,128,512]{2,1,0:T(8,128)(2,1)} %proj_hbm.1, bf16[2,128,128]{2,1,0:T(8,128)(2,1)} %gate_hbm.1, f32[2,128]{1,0:T(2,128)} %out_gain_hbm.1, bf16[2,128,128]{2,1,0:T(8,128)(2,1)} %outw_hbm.1), custom_call_target="tpu_custom_call" | custom-call | tf_op jit(solution)/shard_map/pallas_call | solution.py:462
  61.6 1.9 %copy.9 = bf16[32,64,128]{2,1,0:T(8,128)(2,1)} copy(bf16[32,64,128]{2,1,0:T(8,128)(2,1)} %shard_map.73) | data formatting | bytes 1048576

commit v6 on v5

--- a/solution.py
+++ b/solution.py
@@ -38,7 +38,7 @@
         a, b, c = s % 4, s // 4 % 4, s // 16
         found.append((far[a], far[(a + b) % 4], far[(a + b + c) % 4]))
     found.remove((0, 0, 0))
-    return found
+    return sorted(found, key=lambda offset: -sum((0, 1, 2, 1)[v] for v in offset))
 
 
 def peers():
@@ -52,9 +52,7 @@
 
 def greet(others, core, sibling):
     barrier = pltpu.get_barrier_semaphore()
-    far = [sum((0, 1, 2, 1)[v] for v in offset) for offset in offsets()]
-    for n in sorted(range(CHIPS - 1), key=lambda n: -far[n]):
-        row, col = others[n]
+    for row, col in others:
         pl.semaphore_signal(
             barrier, inc=1, device_id=(row * 2 + core, col), device_id_type=MESH
         )
@@ -111,6 +109,7 @@
     left_m,
     left_k,
     right_m,
+    own_sum,
     in_sem,
     out_sem,
     over_send,
@@ -199,14 +198,16 @@
             right_f[pl.ds(p * 2 + j, C, stride=TILES), :] = right[:, j * 128 : j * 128 + 128]
         gate[p] = sigmoid(times(4))
 
-    def pack(u, part):
-        def step(c, carry):
-            at = pl.ds(pl.multiple_of(c * TILES + part * 8, 8), 8)
-            both = jnp.concatenate([left_f[at, :], right_f[at, :]], axis=0)
-            sides_s[u, part, c] = both.astype(jnp.bfloat16)
+    def pack(u, part, g):
+        def step(row, carry):
+            for col in range(8):
+                c = channel(row, col, g)
+                at = pl.ds(pl.multiple_of(c * TILES + part * 8, 8), 8)
+                both = jnp.concatenate([left_f[at, :], right_f[at, :]], axis=0)
+                sides_s[u, part, c] = both.astype(jnp.bfloat16)
             return carry
 
-        lax.fori_loop(0, C, step, 0, unroll=8)
+        lax.fori_loop(0, 8, step, 0, unroll=4)
 
     def channel(row, col, g):
         return (row * 2 + g) * 8 + col
@@ -227,7 +228,7 @@
     def send_products(u, g):
         sem = 8 + u * 2 + g
         own = channel(half_row, col_index, g)
-        for row, col in others:
+        for row, col in others[::-1] if g == 0 else others:
             pltpu.make_async_remote_copy(
                 prod_s.at[u, g, row * 8 + col],
                 prod_r.at[u, own],
@@ -261,14 +262,15 @@
         return carry
 
     lax.fori_loop(0, PAIRS // 2, first, 0, unroll=4)
-    pack(0, 0)
+    pack(0, 0, 0)
     pl.semaphore_wait(pltpu.get_barrier_semaphore(), CHIPS)
     send_sides(0, 0, 0)
     lax.fori_loop(PAIRS // 2, PAIRS, first, 0, unroll=4)
-    pack(0, 1)
+    pack(0, 1, 0)
     send_sides(0, 0, 1)
-    send_sides(0, 1, 0)
-    send_sides(0, 1, 1)
+    for part in range(PARTS):
+        pack(0, part, 1)
+        send_sides(0, 1, part)
     for n in (5, 6):
         loads[n].wait()
     turn_out(0)
@@ -309,14 +311,14 @@
                             at = pl.multiple_of(part * 128 + q * 16, 16)
                             left_m[g, pl.ds(at, 16), across] = both.astype(jnp.bfloat16)
                         else:
-                            at = pl.multiple_of(part * 256 + core * 128 + q * 16, 16)
+                            at = pl.multiple_of(core * 256 + part * 128 + q * 16, 16)
                             left_k[g, pl.ds(at, 16), across] = both.astype(jnp.bfloat16)
                             both = jnp.concatenate(turned_sides(u, g, part, q, m, 8), axis=0)
                             right_m[1, g, pl.ds(at, 16), across] = both.astype(jnp.bfloat16)
 
                 every(assemble)
                 if u == 1:
-                    rows = pl.ds(pl.multiple_of(part * 256 + core * 128, 128), 128)
+                    rows = pl.ds(pl.multiple_of(core * 256 + part * 128, 128), 128)
                     hand_over(left_k.at[g, rows], 2 + g * 4 + part * 2)
                     hand_over(right_m.at[1, g, rows], 3 + g * 4 + part * 2)
             if u == 0:
@@ -337,6 +339,18 @@
                     hand_over(right_m.at[0, g, pl.ds(at, ROWS)], g)
                 wait_bytes(right_m.at[0, g], over_recv.at[g], 256)
             else:
+
+                def half_product(n, which):
+                    rows = pl.ds(pl.multiple_of(which * 256, 256), 256)
+                    return lax.dot_general(
+                        left_k[g, rows, n * 128 : (n + 1) * 128],
+                        right_m[1, g, rows, :],
+                        (((0,), (0,)), ((), ())),
+                        preferred_element_type=jnp.float32,
+                    )
+
+                for n in range(4):
+                    own_sum[n] = half_product(n, core)
                 for n in range(4):
                     wait_bytes(right_m.at[1, g], over_recv.at[2 + g * 4 + n], 128)
 
@@ -375,12 +389,7 @@
             else:
                 first_core = core == 0
                 for n in range(4):
-                    product = lax.dot_general(
-                        left_k[g, :, n * 128 : (n + 1) * 128],
-                        right_m[1, g],
-                        (((0,), (0,)), ((), ())),
-                        preferred_element_type=jnp.float32,
-                    )
+                    product = own_sum[n] + half_product(n, 1 - core)
                     for q in range(2):
                         for m in range(4):
                             across = slice(m * 128, (m + 1) * 128)
@@ -435,13 +444,14 @@
             lax.fori_loop(part * 4, part * 4 + 4, finish, 0, unroll=4)
             if u == 0:
                 lax.fori_loop(part * 4, part * 4 + 4, second, 0, unroll=4)
-                pack(1, part)
+                pack(1, part, 0)
                 send_sides(1, 0, part)
             else:
                 for h in range(2):
                     stores[part * 2 + h].start()
         if u == 0:
             for part in range(PARTS):
+                pack(1, part, 1)
                 send_sides(1, 1, part)
 
     for u in range(2):
@@ -490,6 +500,7 @@
             pltpu.VMEM((2, 256, 512), jnp.bfloat16),
             pltpu.VMEM((2, 512, 512), jnp.bfloat16),
             pltpu.VMEM((2, 2, 512, 512), jnp.bfloat16),
+            pltpu.VMEM((4, 128, 512), jnp.float32),
             pltpu.SemaphoreType.DMA((7,)),
             pltpu.SemaphoreType.DMA((4,)),
             pltpu.SemaphoreType.DMA((10,)),

time: 63.6 us -> 60.8 us (0.956)
  Pallas kernels: 61.5 us -> 58.8 us
    pallas_call x1, Pallas kernels: 61.5 us -> 58.8 us  [shards(): pl.pallas_call(kernel, out_shape=jax.ShapeDtypeStruct(pair.shape, pair.dt...]
where the time goes in v6:
time: 60.8 us; the launch traced here: 60.6 us
  Pallas kernels  58.8 us (97%)
  local copies, waits for them, and re-layouts  1.87 us (3%)
    pallas_call x1, Pallas kernels, shards(): pl.pallas_call(kernel, out_shape=jax.ShapeDtypeStruct(pair.shape, pair.dt...  58.8 us
    unnamed x1, local copies, waits for them, and re-layouts  1.87 us

profile of v6, /device:TPU:1, one launch (start us, length us, event | category | flops | bytes accessed | tf_op | source)
XLA Modules:
  0.0 60.6 jit_solution(4767856285062923054)
XLA Ops:
  0.0 58.8 %shard_map.73 = bf16[32,64,128]{2,1,0:T(8,128)(2,1)} custom-call(s32[512]{0:T(512)} %mask_hbm.1, bf16[32,64,128]{2,1,0:T(8,128)(2,1)} %pair_hbm.1, f32[2,128]{1,0:T(2,128)} %in_gain_hbm.1, bf16[2,128,512]{2,1,0:T(8,128)(2,1)} %proj_hbm.1, bf16[2,128,128]{2,1,0:T(8,128)(2,1)} %gate_hbm.1, f32[2,128]{1,0:T(2,128)} %out_gain_hbm.1, bf16[2,128,128]{2,1,0:T(8,128)(2,1)} %outw_hbm.1), custom_call_target="tpu_custom_call" | custom-call | tf_op jit(solution)/shard_map/pallas_call | solution.py:472
  58.8 1.9 %copy.9 = bf16[32,64,128]{2,1,0:T(8,128)(2,1)} copy(bf16[32,64,128]{2,1,0:T(8,128)(2,1)} %shard_map.73) | data formatting | bytes 1048576

commit v7 on v6

--- a/solution.py
+++ b/solution.py
@@ -204,7 +204,7 @@
                 c = channel(row, col, g)
                 at = pl.ds(pl.multiple_of(c * TILES + part * 8, 8), 8)
                 both = jnp.concatenate([left_f[at, :], right_f[at, :]], axis=0)
-                sides_s[u, part, c] = both.astype(jnp.bfloat16)
+                sides_s[u, c, part] = both.astype(jnp.bfloat16)
             return carry
 
         lax.fori_loop(0, 8, step, 0, unroll=4)
@@ -214,16 +214,17 @@
 
     def send_sides(u, g, part):
         sem = (u * 2 + g) * 2 + part
+        at = slice(None) if g == 1 else part
         for row, col in others:
             pltpu.make_async_remote_copy(
-                sides_s.at[u, part, channel(row, col, g)],
-                sides_r.at[u, g, part, chip],
+                sides_s.at[u, channel(row, col, g), at],
+                sides_r.at[u, g, chip, at],
                 send_sem.at[sem],
                 recv_sem.at[sem],
                 device_id=(row * 2 + core, col),
                 device_id_type=MESH,
             ).start()
-        sides_r[u, g, part, chip] = sides_s[u, part, channel(half_row, col_index, g)]
+        sides_r[u, g, chip, at] = sides_s[u, channel(half_row, col_index, g), at]
 
     def send_products(u, g):
         sem = 8 + u * 2 + g
@@ -270,7 +271,7 @@
     send_sides(0, 0, 1)
     for part in range(PARTS):
         pack(0, part, 1)
-        send_sides(0, 1, part)
+    send_sides(0, 1, 0)
     for n in (5, 6):
         loads[n].wait()
     turn_out(0)
@@ -291,7 +292,7 @@
 
     def turned_sides(u, g, part, q, m, side):
         tiles = [
-            sides_r[u, g, part, q * 8 + 2 * m + j][side : side + 8, :].astype(jnp.float32)
+            sides_r[u, g, q * 8 + 2 * m + j, part][side : side + 8, :].astype(jnp.float32)
             for j in range(2)
         ]
         return swap(tiles[0], tiles[1])
@@ -299,9 +300,10 @@
     for u in range(2):
         for g in range(2):
             for part in range(PARTS):
-                wait_bytes(
-                    sides_r.at[u, g, part], recv_sem.at[(u * 2 + g) * 2 + part], CHIPS - 1
-                )
+                if g == 0:
+                    wait_bytes(prod_r.at[u], recv_sem.at[u * 4 + part], CHIPS - 1)
+                elif part == 0:
+                    wait_bytes(sides_r.at[u, g], recv_sem.at[u * 4 + 2], CHIPS - 1)
 
                 def assemble(q):
                     for m in range(4):
@@ -452,13 +454,15 @@
         if u == 0:
             for part in range(PARTS):
                 pack(1, part, 1)
-                send_sides(1, 1, part)
+            send_sides(1, 1, 0)
 
     for u in range(2):
         for g in range(2):
-            for part in range(PARTS):
-                sem = (u * 2 + g) * 2 + part
-                wait_bytes(sides_r.at[u, g, part], send_sem.at[sem], CHIPS - 1)
+            if g == 0:
+                for part in range(PARTS):
+                    wait_bytes(prod_r.at[u], send_sem.at[u * 4 + part], CHIPS - 1)
+            else:
+                wait_bytes(sides_r.at[u, g], send_sem.at[u * 4 + 2], CHIPS - 1)
             wait_bytes(prod_s.at[u, g], send_sem.at[8 + u * 2 + g], CHIPS - 1)
     for g in range(2):
         wait_bytes(right_m.at[0, g], over_send.at[g], 256)
@@ -492,8 +496,8 @@
             pltpu.VMEM((PAIRS, 128, 256), jnp.float32),
             pltpu.VMEM((C * TILES, 128), jnp.float32),
             pltpu.VMEM((C * TILES, 128), jnp.float32),
-            pltpu.VMEM((2, PARTS, C, 16, 128), jnp.bfloat16),
-            pltpu.VMEM((2, 2, PARTS, CHIPS, 16, 128), jnp.bfloat16),
+            pltpu.VMEM((2, C, PARTS, 16, 128), jnp.bfloat16),
+            pltpu.VMEM((2, 2, CHIPS, PARTS, 16, 128), jnp.bfloat16),
             pltpu.VMEM((2, 2, CHIPS, 16, 128), jnp.bfloat16),
             pltpu.VMEM((2, C, 16, 128), jnp.bfloat16),
             pltpu.VMEM((C * TILES, 128), jnp.float32),

time: 60.8 us -> 61.8 us (1.016)
  Pallas kernels: 58.8 us -> 59.8 us
    pallas_call x1, Pallas kernels: 58.8 us -> 59.8 us  [shards(): pl.pallas_call(kernel, out_shape=jax.ShapeDtypeStruct(pair.shape, pair.dt...]
where the time goes in v7:
time: 61.8 us; the launch traced here: 61.7 us
  Pallas kernels  59.8 us (97%)
  local copies, waits for them, and re-layouts  1.87 us (3%)
    pallas_call x1, Pallas kernels, shards(): pl.pallas_call(kernel, out_shape=jax.ShapeDtypeStruct(pair.shape, pair.dt...  59.8 us
    unnamed x1, local copies, waits for them, and re-layouts  1.87 us

profile of v7, /device:TPU:1, one launch (start us, length us, event | category | flops | bytes accessed | tf_op | source)
XLA Modules:
  0.0 61.7 jit_solution(9633311862921246838)
XLA Ops:
  0.0 59.8 %shard_map.73 = bf16[32,64,128]{2,1,0:T(8,128)(2,1)} custom-call(s32[512]{0:T(512)} %mask_hbm.1, bf16[32,64,128]{2,1,0:T(8,128)(2,1)} %pair_hbm.1, f32[2,128]{1,0:T(2,128)} %in_gain_hbm.1, bf16[2,128,512]{2,1,0:T(8,128)(2,1)} %proj_hbm.1, bf16[2,128,128]{2,1,0:T(8,128)(2,1)} %gate_hbm.1, f32[2,128]{1,0:T(2,128)} %out_gain_hbm.1, bf16[2,128,128]{2,1,0:T(8,128)(2,1)} %outw_hbm.1), custom_call_target="tpu_custom_call" | custom-call | tf_op jit(solution)/shard_map/pallas_call | solution.py:476
  59.8 1.9 %copy.9 = bf16[32,64,128]{2,1,0:T(8,128)(2,1)} copy(bf16[32,64,128]{2,1,0:T(8,128)(2,1)} %shard_map.73) | data formatting | bytes 1048576
